TPU v7x, 32 devices: a whole 2x2x4 slice. The times are simulated.
32 devices in a mesh: ctx: 8 (over y, x, core), img: 4 (over z).
Axes of the slice: x: 2, y: 2, z: 4, core: 2. Of those that a mesh axis runs over, the one named last changes fastest.
Arguments:
- text: bfloat16 [1024, 4096], P('ctx'), may hold values from -6 to 6
- input_gain: float32 [4096], replicated, may hold values from 0.5 to 2
- q_weight: bfloat16 [4096, 4096], P('ctx', 'img'), may hold values from -0.09375 to 0.09375
- kv_weight: bfloat16 [4096, 2048], P('ctx'), may hold values from -0.09375 to 0.09375
- o_weight: bfloat16 [4096, 4096], P('img', 'ctx'), may hold values from -0.5 to 0.5
- q_gain: float32 [128], replicated, may hold values from 0.5 to 12, as said below
- k_gain: float32 [128], replicated, may hold values from 0.5 to 12, as said below
- attn_gate: float32 [1], replicated, may hold values from 0.3 to 1.5
- vision: bfloat16 [8, 64, 4096], P('img', 'ctx'), may hold values from -6 to 6
- segment_ids: int32 [1024], P('ctx'), may hold values from 0 to 31, as said below
- seg_images: int32 [32, 2], replicated, may hold values from 0 to 7, as said below
- image_slot: int32 [8], replicated, may hold values from 0 to 7, each once
Outputs:
- mixed: bfloat16 [1024, 4096], P('ctx', 'img')
Inputs may be any that keep to these rules, and one draw needn't show every extreme that they name: `segment_ids`: numbers never fall along the tokens; block c of 128 tokens uses numbers from c * 4 on, 1 to 4 segments a block, and some block has 4. `seg_images`: each row names 2 different images; the tokens of one block of 128 see at most 8 different images, and some block sees exactly 8. `image_slot`: A permutation. `q_gain`: Positive. `k_gain`: Positive.
All inputs are finite; a program needn't handle non-finite values.
Results may differ from a plain program's by a relative error of at most 0.022.
The roundings to bfloat16 on the way count: a program that leaves them out, or rounds other values in their place, can miss the bound.
Values may be sent and summed in bfloat16 or wider, within the bound.
No kernel may reach another device: no remote copies, remote signals or barrier semaphores. Data moves between devices by JAX's collectives and lax.ppermute only.
A program may use at most 64 MiB of HBM per device.

v0:
```python
import jax
import jax.numpy as jnp
from jax import lax
from jax.experimental import pallas as pl
from jax.experimental.pallas import tpu as pltpu
from jax.sharding import PartitionSpec as P

KVH = 8


EPS = 1e-05
NEG = -1e30


def head_norm(values, gain):
    mean_sq = jnp.mean(values * values, axis=-1, keepdims=True)
    return values * lax.rsqrt(mean_sq + EPS) * gain


def attend(query, keys, values, mask):
    scale = query.shape[-1] ** (-0.5)
    scores = jnp.einsum("tkgd,nkd->tkgn", query, keys, preferred_element_type=jnp.float32) * scale
    live = mask[:, None, None, :]
    scores = jnp.where(live, scores, NEG)
    top = jnp.max(scores, axis=-1)
    weights = jnp.where(live, jnp.exp(scores - top[..., None]), 0.0)
    total = jnp.sum(weights, axis=-1)
    acc = jnp.einsum(
        "tkgn,nkd->tkgd", weights.astype(jnp.bfloat16), values, preferred_element_type=jnp.float32
    )
    return acc / total[..., None]


def general(
    text,
    input_gain,
    q_weight,
    kv_weight,
    o_weight,
    q_gain,
    k_gain,
    attn_gate,
    vision,
    segment_ids,
    seg_images,
    image_slot,
):
    tokens_here = text.shape[0]
    head_dim = q_gain.shape[0]
    ctx_count = lax.axis_size("ctx")
    img_count = lax.axis_size("img")
    heads_here = q_weight.shape[1] // head_dim
    kv_heads = max(1, KVH // img_count)
    group = heads_here // kv_heads
    slots_here, vt_dev = vision.shape[:2]
    rows_here = slots_here * vt_dev

    o_full = lax.all_gather(o_weight, "ctx", axis=1, tiled=True)
    vision_cols = lax.all_to_all(
        vision.reshape(rows_here, -1), "ctx", split_axis=1, concat_axis=0, tiled=True
    )
    hidden = head_norm(text.astype(jnp.float32), input_gain).astype(jnp.bfloat16)
    hidden_cols = lax.all_to_all(hidden, "ctx", split_axis=1, concat_axis=0, tiled=True)

    kv_share = jnp.dot(vision_cols, kv_weight, preferred_element_type=jnp.float32)
    kv_shares = lax.all_to_all(
        kv_share.reshape(ctx_count, rows_here, -1), "ctx", split_axis=0, concat_axis=0, tiled=True
    )
    projected = jnp.sum(kv_shares, axis=0).reshape(rows_here, KVH, 2, head_dim)
    keys = head_norm(projected[:, :, 0], k_gain).astype(jnp.bfloat16)
    values = projected[:, :, 1].astype(jnp.bfloat16)
    kv_rows = jnp.stack((keys, values), axis=2)
    owners = jnp.arange(img_count)[:, None] * KVH // img_count + jnp.arange(kv_heads)[None, :]
    kv_out = jnp.take(kv_rows, owners, axis=1).transpose(1, 0, 2, 3, 4)
    kv_in = lax.all_to_all(kv_out, "img", split_axis=0, concat_axis=0, tiled=True)
    kv_all = lax.all_gather(kv_in, "ctx", axis=0, tiled=False)

    q_share = jnp.dot(hidden_cols, q_weight, preferred_element_type=jnp.float32)
    q_shares = lax.all_to_all(
        q_share.astype(jnp.bfloat16).reshape(ctx_count, tokens_here, -1),
        "ctx",
        split_axis=0,
        concat_axis=0,
        tiled=True,
    )
    query = jnp.sum(q_shares.astype(jnp.float32), axis=0)
    query = head_norm(query.reshape(tokens_here, kv_heads, group, head_dim), q_gain).astype(
        jnp.bfloat16
    )

    slots = img_count * slots_here
    own_slots = jnp.take(image_slot, jnp.take(seg_images, segment_ids, axis=0), axis=0)
    slot_ids = jnp.arange(slots, dtype=jnp.int32)
    sees = jnp.any(own_slots[:, :, None] == slot_ids[None, None, :], axis=1)
    flat = kv_all.reshape(ctx_count * slots * vt_dev, kv_heads, 2, head_dim)
    mask = jnp.broadcast_to(
        sees[:, None, :, None], (tokens_here, ctx_count, slots, vt_dev)
    ).reshape(tokens_here, -1)
    context = attend(query, flat[:, :, 0], flat[:, :, 1], mask)
    context = context.astype(jnp.bfloat16).reshape(tokens_here, heads_here * head_dim)
    partial_terms = jnp.dot(context, o_full, preferred_element_type=jnp.float32)
    width = partial_terms.shape[1] // img_count
    shares = lax.all_to_all(
        partial_terms.astype(jnp.bfloat16).reshape(tokens_here, img_count, width),
        "img",
        split_axis=1,
        concat_axis=1,
        tiled=True,
    )
    update = jnp.sum(shares.astype(jnp.float32), axis=1)
    own_text = lax.dynamic_slice_in_dim(text, lax.axis_index("img") * width, width, 1)
    return (own_text.astype(jnp.float32) + jnp.tanh(attn_gate[0]) * update).astype(jnp.bfloat16)


BF16, F32 = jnp.bfloat16, jnp.float32
SMEM = pl.BlockSpec(memory_space=pltpu.SMEM)
VMEM = pl.BlockSpec(memory_space=pltpu.VMEM)
CHIPS = 4


def call(kernel, args, specs, outs, out_specs=None, scratch=(), flops=0, size=0, name=None, grid=(), limit=24):
    return pl.pallas_call(
        kernel,
        out_shape=outs,
        in_specs=specs,
        out_specs=[VMEM] * len(outs) if out_specs is None else out_specs,
        scratch_shapes=scratch,
        grid=grid,
        compiler_params=pltpu.CompilerParams(vmem_limit_bytes=limit * 2**20),
        cost_estimate=pl.CostEstimate(flops=flops, bytes_accessed=size, transcendentals=0),
        name=name,
    )(*args)


def block(index, size):
    return pl.ds(pl.multiple_of(index * size, size), size)


def row_scales(text, scale, step, ready=()):
    for k, r in enumerate(range(0, text.shape[0], step)):
        if ready:
            ready[k].wait()
        x = text[r : r + step, :].astype(F32)
        mean_sq = jnp.mean(x * x, axis=-1, keepdims=True)
        scale[r : r + step, :] = jnp.broadcast_to(lax.rsqrt(mean_sq + EPS), (step, 128))


def scaled(text, scale, gain, out, index, step):
    cols = block(index, out.shape[1])
    row_gain = gain[:, cols]
    for r in range(0, text.shape[0], step):
        x = text[r : r + step, cols].astype(F32)
        out[r : r + step, :] = (x * scale[r : r + step, 0:1] * row_gain).astype(BF16)


def start_kernel(where, text_hbm, gain, vis_hbm, q_hbm, *refs):
    pieces, refs = refs[:CHIPS], refs[CHIPS:]
    far, q_keep, q_give, text, vis, scale, sems = refs
    chip, core = where[0], where[1]
    tokens = text.shape[0]
    half = q_keep.shape[1]
    step = 16
    first = pltpu.make_async_copy(vis_hbm, vis, sems.at[0])
    first.start()
    copies = []
    for k, r in enumerate(range(0, tokens, step)):
        rows = pl.ds(r, step)
        copies.append(pltpu.make_async_copy(text_hbm.at[rows, :], text.at[rows, :], sems.at[3 + k]))
        copies[-1].start()
    cuts = [
        pltpu.make_async_copy(q_hbm.at[:, block(core, half)], q_keep, sems.at[1]),
        pltpu.make_async_copy(q_hbm.at[:, block(1 - core, half)], q_give, sems.at[2]),
    ]
    for copy in cuts:
        copy.start()
    first.wait()
    for s in range(CHIPS):
        pieces[s][...] = vis[:, block(chip ^ s, pieces[s].shape[1])]
    row_scales(text, scale, step, copies)
    scaled(text, scale, gain, far, 1 - chip // 2, step)
    for copy in cuts:
        copy.wait()


def near_kernel(where, text, gain, near, text_keep, text_give, scale):
    chip, core, plane = where[0], where[1], where[2]
    half = text_keep.shape[1]
    row_scales(text, scale, 16)
    scaled(text, scale, gain, near, chip // 2, 16)
    text_keep[...] = text[:, block(2 * plane + core, half)]
    text_give[...] = text[:, block(2 * plane + 1 - core, half)]


def kv_kernel(where, *refs):
    vis, vis_other, refs = refs[:CHIPS], refs[CHIPS : 2 * CHIPS], refs[2 * CHIPS :]
    (kv_own, kv_other), refs = refs[:2], refs[2:]
    shares, (other, near_total, sems) = refs[:CHIPS], refs[CHIPS:]
    core = where[1]
    rows = kv_own.shape[0]
    head = kv_own.shape[1] // (2 * CHIPS)
    copies = []
    for j in range(CHIPS):
        copies.append(
            pltpu.make_async_copy(
                kv_other.at[:, block(2 * j + core, head)],
                other.at[:, pl.ds(j * head, head)],
                sems.at[j],
            )
        )
        copies[-1].start()
    near, far = block(core, rows), block(1 - core, rows)
    x_near = jnp.concatenate([x[:, near] for x in vis + vis_other], axis=0)
    x_far = jnp.concatenate([x[:, far] for x in vis + vis_other], axis=0)
    count = vis[0].shape[0]
    total = CHIPS * count
    for j in range(CHIPS):
        near_total[:, j * head : (j + 1) * head] = jnp.dot(
            x_near, kv_own[:, block(2 * j + core, head)], preferred_element_type=F32
        )
    for j in range(CHIPS):
        copies[j].wait()
        cols = slice(j * head, (j + 1) * head)
        out = near_total[:, cols] + jnp.dot(x_far, other[:, cols], preferred_element_type=F32)
        for s in range(CHIPS):
            shares[s][:count, cols] = out[s * count : (s + 1) * count]
            shares[s][count:, cols] = out[total + s * count : total + (s + 1) * count]


def kv_norm_kernel(where, k_gain, *refs):
    shares, (here, there, give) = refs[:CHIPS], refs[CHIPS:]
    plane = where[2]
    lines, head = here.shape
    dim = head // 2
    for t, (out, row) in enumerate(((here, 0), (give, 0), (there, 0), (give, lines))):
        cols = block(plane ^ t, head)
        total = (shares[0][:, cols] + shares[1][:, cols]) + (shares[2][:, cols] + shares[3][:, cols])
        keys = head_norm(total[:, :dim], k_gain[...])
        out[row : row + lines, :dim] = keys.astype(BF16)
        out[row : row + lines, dim:] = total[:, dim:].astype(BF16)


def kv_turn_kernel(there, landed, out):
    lines = there.shape[0]
    out[:lines, :] = there[...]
    out[lines:, :] = landed[lines:, :]


def kv_join_kernel(here, landed, last, out):
    lines = here.shape[0]
    out[:lines, :] = here[...]
    out[lines : 2 * lines, :] = landed[:lines, :]
    out[2 * lines :, :] = last[...]


def query_share(index, own, other, first, second, flip):
    rows = first.shape[0]
    total = None
    for weight, k in ((first, index), (second, index ^ flip)):
        cols = block(k, rows)
        x = jnp.concatenate((own[:, cols], other[:, cols]), axis=0)
        share = jnp.dot(x, weight[...], preferred_element_type=F32)
        total = share if total is None else total + share
    return total


def early_kernel(where, own, other, q_keep, q_other, out):
    index = 2 * lax.rem(where[0], 2) + where[1]
    out[...] = query_share(index, own, other, q_keep, q_other, 1)


def late_kernel(where, own, other, q_side, q_corner, early, out):
    index = (2 * lax.rem(where[0], 2) + where[1]) ^ 2
    share = early[...] + query_share(index, own, other, q_side, q_corner, 1)
    out[...] = share.astype(out.dtype)


def attend_kernel(q_gain, first, landed, *refs):
    kv, (bias, context) = refs[:CHIPS], refs[CHIPS:]
    dim = q_gain.shape[1]
    rows, half = context.shape
    keys = jnp.concatenate([x[:, :dim] for x in kv], axis=0)
    values = jnp.concatenate([x[:, dim:] for x in kv], axis=0)
    step = 128
    for r in range(0, rows, step):
        for g in range(half // dim):
            cols = slice(g * dim, (g + 1) * dim)
            query = first[r : r + step, cols] + landed[r : r + step, cols].astype(F32)
            query = head_norm(query, q_gain[...]).astype(BF16)
            scores = lax.dot_general(
                query, keys, (((1,), (1,)), ((), ())), preferred_element_type=F32
            )
            scores = scores * dim ** (-0.5) + bias[r : r + step, :]
            weights = jnp.exp(scores - jnp.max(scores, axis=-1, keepdims=True))
            total = jnp.sum(weights, axis=-1, keepdims=True)
            acc = jnp.dot(weights.astype(BF16), values, preferred_element_type=F32)
            context[r : r + step, cols] = (acc / total).astype(BF16)


def out_kernel(where, near, far, o_own, o_early, o_late, own, other):
    core = where[1]
    tokens, width = own.shape
    half = near.shape[1]
    turned = jnp.concatenate((far[tokens:, :], far[:tokens, :]), axis=0)
    share = jnp.dot(near[...], o_own[block(core, half), :], preferred_element_type=F32)
    share += jnp.dot(turned, o_own[block(1 - core, half), :], preferred_element_type=F32)
    own[:, : width // 2] = share[:tokens].astype(BF16)
    other[:, : width // 2] = share[tokens:].astype(BF16)
    top = jnp.where(core == 0, near[...], turned)
    low = jnp.where(core == 0, turned, near[...])
    share = jnp.dot(top, o_early[...], preferred_element_type=F32)
    share += jnp.dot(low, o_late[...], preferred_element_type=F32)
    own[:, width // 2 :] = share[:tokens].astype(BF16)
    other[:, width // 2 :] = share[tokens:].astype(BF16)


def pick_kernel(where, own, landed, *outs):
    first = where[0] ^ where[2]
    half = outs[0].shape[1]
    for t in range(CHIPS):
        for s in range(CHIPS):

            @pl.when((first ^ t) == s)
            def _():
                outs[t][...] = (own, landed)[s % 2][:, (s // 2) * half : (s // 2 + 1) * half]


def mixed_rows(gate, text, shares):
    x = [share[...].astype(F32) for share in shares]
    update = (x[0] + x[1]) + (x[2] + x[3])
    return (text[...].astype(F32) + gate[0] * update).astype(BF16)


def give_kernel(gate, text, *refs):
    refs[CHIPS][...] = mixed_rows(gate, text, refs[:CHIPS])


def last_kernel(where, gate, text, back, *refs):
    shares, out = refs[:CHIPS], refs[CHIPS]
    core = where[1]
    half = text.shape[1]
    out[:, block(core, half)] = mixed_rows(gate, text, shares)
    out[:, block(1 - core, half)] = back[...]


def paired(
    text,
    input_gain,
    q_weight,
    kv_weight,
    o_weight,
    q_gain,
    k_gain,
    attn_gate,
    vision,
    segment_ids,
    seg_images,
    image_slot,
):
    ctx_count = lax.axis_size("ctx")
    place, plane = lax.axis_index("ctx"), lax.axis_index("img")
    chip, core = place // 2, place % 2
    where = jnp.stack((chip, core, plane)).astype(jnp.int32)
    tokens, width = text.shape
    head_dim = q_gain.shape[0]
    rows_dev, cols_plane = q_weight.shape
    half = cols_plane // 2
    part = 2 * rows_dev
    slots_here, vt_dev = vision.shape[:2]
    vis_here = slots_here * vt_dev
    kv_cols = kv_weight.shape[1] // 2

    def shape(rows, cols, kind=BF16):
        return jax.ShapeDtypeStruct((rows, cols), kind)

    def swap(x):
        return lax.ppermute(x, "ctx", [(k, k ^ 1) for k in range(ctx_count)])

    def peer(x, s):
        return lax.ppermute(x, "ctx", [(k, k ^ (2 * s)) for k in range(ctx_count)])

    def along_x(x):
        return peer(x, 1)

    def along_y(x):
        return peer(x, 2)

    def across(x, t):
        return lax.ppermute(x, "img", [(k, k ^ t) for k in range(CHIPS)])

    steps = range(1, CHIPS)
    vis = vision.reshape(vis_here, width)
    kv_other = swap(kv_weight)

    anywhere = pl.BlockSpec(memory_space=pl.ANY)
    *vis_pieces, far, q_keep, q_give = call(
        start_kernel,
        (where, text, input_gain[None], vis, q_weight),
        [SMEM, anywhere, VMEM, anywhere, anywhere],
        [shape(vis_here, part)] * CHIPS
        + [shape(tokens, width // 2)]
        + [shape(rows_dev, half)] * 2,
        out_specs=[VMEM] * (1 + CHIPS) + [anywhere] * 2,
        scratch=[
            pltpu.VMEM((tokens, width), BF16),
            pltpu.VMEM((vis_here, width), BF16),
            pltpu.VMEM((tokens, 128), F32),
            pltpu.SemaphoreType.DMA((3 + tokens // 16,)),
        ],
        flops=8 * tokens * width,
        size=4 * 2**20,
        name="start",
        limit=60,
    )
    vis_own = [vis_pieces[0]] + [peer(vis_pieces[s], s) for s in steps]
    vis_other = [swap(x) for x in vis_own]
    q_side, q_other = along_x(q_keep), swap(q_give)
    far = along_y(far)

    shares = call(
        kv_kernel,
        (where, *vis_own, *vis_other, kv_weight, kv_other),
        [SMEM] + [VMEM] * (1 + 2 * CHIPS) + [pl.BlockSpec(memory_space=pl.ANY)],
        [shape(2 * vis_here, kv_cols, F32)] * CHIPS,
        scratch=[
            pltpu.VMEM((rows_dev, kv_cols), BF16),
            pltpu.VMEM((8 * vis_here, kv_cols), F32),
            pltpu.SemaphoreType.DMA((CHIPS,)),
        ],
        flops=4 * vis_here * ctx_count * part * kv_cols,
        size=4 * 2**20,
        name="kv_shares",
    )
    where_near, _ = lax.optimization_barrier((where, shares[0]))
    near, text_keep, text_give = call(
        near_kernel,
        (where_near, text, input_gain[None]),
        [SMEM, VMEM, VMEM],
        [shape(tokens, width // 2)] + [shape(tokens, half)] * 2,
        scratch=[pltpu.VMEM((tokens, 128), F32)],
        flops=8 * tokens * width,
        size=4 * 2**20,
        name="near",
    )
    shares = [shares[0]] + [peer(shares[s], s) for s in steps]
    shares[3], q_side, far, near = lax.optimization_barrier((shares[3], q_side, far, near))
    here, there, give = call(
        kv_norm_kernel,
        (where, k_gain[None], *shares),
        [SMEM] + [VMEM] * (1 + CHIPS),
        [shape(2 * vis_here, 2 * head_dim)] * 2 + [shape(4 * vis_here, 2 * head_dim)],
        name="kv_norm",
    )
    blocks = ((far, swap(far)), (near, swap(near)))
    early = [
        call(
            early_kernel,
            (where, *pair, q_keep, q_other),
            [SMEM] + [VMEM] * 4,
            [shape(2 * tokens, half, F32)],
            flops=4 * tokens * part * half,
            size=2 * 2**20,
            name="q_early",
        )[0]
        for pair in blocks
    ]
    kv_z = across(give, 1)
    kv_z, early[0] = lax.optimization_barrier((kv_z, early[0]))
    turn = call(
        kv_turn_kernel,
        (there, kv_z),
        [VMEM] * 2,
        [shape(4 * vis_here, 2 * head_dim)],
        name="kv_turn",
    )[0]
    kv_first = call(
        kv_join_kernel,
        (here, kv_z, across(turn, 2)),
        [VMEM] * 3,
        [shape(8 * vis_here, 2 * head_dim)],
        name="kv_join",
    )[0]
    kv_all = [kv_first] + [peer(kv_first, s) for s in steps]

    q_behind, _ = lax.optimization_barrier((q_other, shares[0]))
    q_corner = along_x(q_behind)

    o_early, _ = lax.optimization_barrier((o_weight[:half], here))
    q_corner, o_early = lax.optimization_barrier((q_corner, along_y(o_early)))
    early[1], kv_all[1] = lax.optimization_barrier((early[1], kv_all[1]))
    q_far, q_first = [
        call(
            late_kernel,
            (where, *blocks[k], q_side, q_corner, early[k]),
            [SMEM] + [VMEM] * 5,
            [shape(2 * tokens, half, kind)],
            flops=4 * tokens * part * half,
            size=2 * 2**20,
            name="q_late",
        )[0]
        for k, kind in ((0, BF16), (1, F32))
    ]
    landed = along_y(q_far)
    o_late, _ = lax.optimization_barrier((o_weight[half:], q_far))
    o_late = along_y(o_late)

    ids = jnp.concatenate((segment_ids, swap(segment_ids)))
    images = jnp.arange(image_slot.shape[0])
    slot_of = jnp.sum(
        jnp.where(seg_images[:, :, None] == images, image_slot[None, None, :], 0), axis=2
    )
    numbers = jnp.arange(seg_images.shape[0])
    own_slots = jnp.sum(
        jnp.where((ids[:, None] == numbers)[:, :, None], slot_of[None], 0), axis=1
    )
    key_rows = jnp.arange(CHIPS * CHIPS * 2 * vis_here)
    key_plane = plane ^ (key_rows // (2 * vis_here) % CHIPS)
    key_slot = key_plane * slots_here + key_rows // vt_dev % slots_here
    sees = jnp.any(own_slots[:, :, None] == key_slot, axis=1)
    bias = jnp.where(sees, 0.0, NEG).astype(F32)

    context = call(
        attend_kernel,
        (q_gain[None], q_first, landed, *kv_all, bias),
        [VMEM] * (4 + CHIPS),
        [shape(2 * tokens, half)],
        flops=8 * tokens * half * bias.shape[1],
        size=2 * 2**20,
        name="attend",
    )[0]

    context_x = along_x(context)
    shares = [
        call(
            out_kernel,
            (where, x, swap(x), o_weight, o_early, o_late),
            [SMEM] + [VMEM] * 5,
            [shape(tokens, 2 * half)] * 2,
            flops=8 * tokens * cols_plane * half,
            size=2 * 2**20,
            name="o_share",
        )
        for x in (context_x, context)
    ]
    summands = []
    for rows in (1, 0):
        picked = call(
            pick_kernel,
            (where, shares[1][rows], along_x(shares[0][rows])),
            [SMEM] + [VMEM] * 2,
            [shape(tokens, half)] * CHIPS,
            flops=2**20,
            size=2**20,
            name="pick",
        )
        summands.append([picked[0]] + [across(picked[t], t) for t in steps])
    gate = jnp.tanh(attn_gate)
    give = call(
        give_kernel,
        (gate, swap(text_give), *summands[0]),
        [SMEM] + [VMEM] * (1 + CHIPS),
        [shape(tokens, half)],
        flops=2**20,
        size=2**20,
        name="mix_give",
    )[0]
    return call(
        last_kernel,
        (where, gate, text_keep, swap(give), *summands[1]),
        [SMEM, SMEM] + [VMEM] * (2 + CHIPS),
        [shape(tokens, 2 * half)],
        flops=2**20,
        size=2**20,
        name="mix_keep",
    )[0]


def solution(mesh):
    fits = mesh.shape["img"] == 4 and mesh.shape["ctx"] == 8
    return jax.shard_map(
        paired if fits else general,
        mesh=mesh,
        in_specs=(
            P("ctx", None),
            P(),
            P("ctx", "img"),
            P("ctx", None),
            P("img", "ctx"),
            P(),
            P(),
            P(),
            P("img", "ctx", None),
            P("ctx"),
            P(),
            P(),
        ),
        out_specs=P("ctx", "img"),
        check_vma=False,
    )
```

profile of v0, /device:TPU:0, one launch (start us, length us, event | category | flops | bytes accessed | tf_op | source)
XLA Modules:
  0.0 146.7 jit_solution(397361859664401044)
XLA Ops:
  1.1 34.6 %start.1 = (bf16[16,1024]{1,0:T(8,128)(2,1)}, bf16[16,1024]{1,0:T(8,128)(2,1)}, bf16[16,1024]{1,0:T(8,128)(2,1)}, bf16[16,1024]{1,0:T(8,128)(2,1)}, bf16[128,204...) custom-call(s32[3]{0:T(128)} %pad_add_fusion.1.where, bf16[128,4096]{1,0:T(8,128)(2,1)} %text.1, ...), custom_call_target="tpu_custom_call" | custom-call | flops 4194304 | bytes 4194304 | tf_op jit(solution)/shard_map/start/pallas_call | solution.py:122
  35.7 2.6 %collective-permute-start.10 = (bf16[512,512]{1,0:T(8,128)(2,1)}, bf16[512,512]{1,0:T(8,128)(2,1)S(1)}, u32[]{:S(2)}, u32[]{:S(2)}) collective-permute-start(bf16[512,512]{1,0:T(8,128)(2,1)} %get-tuple-element.57.q_keep), channel_id=1, source_target_pairs={{0,8},{4,12},{8,0},{12,4},{16,24},{20,28},{24,16},{28,20},{1,9},{5... | collective-permute-start | bytes 1572872 | tf_op jit(solution)/shard_map/ppermute | solution.py:379
  38.3 2.0 %collective-permute-start.1 = (bf16[16,1024]{1,0:T(8,128)(2,1)}, bf16[16,1024]{1,0:T(8,128)(2,1)S(1)}, u32[]{:S(2)}, u32[]{:S(2)}) collective-permute-start(bf16[16,1024]{1,0:T(8,128)(2,1)} %get-tuple-element.50), channel_id=1, source_target_pairs={{0,16},{4,20},{8,24},{12,28},{16,0},{20,4},{24,8},{28,12},{1,17},{... | collective-permute-start | bytes 98312 | tf_op jit(solution)/shard_map/ppermute | solution.py:379
  40.3 1.4 collective-permute-start.2
  41.7 10.2 %collective-permute-done.refs_1_ = bf16[16,1024]{1,0:T(8,128)(2,1)S(1)} collective-permute-done((bf16[16,1024]{1,0:T(8,128)(2,1)}, bf16[16,1024]{1,0:T(8,128)(2,1)S(1)}, u32[]{:S(2)}, u32[]{:S(2)}) %collective-permute-start) | collective-permute-done | bytes 32800 | tf_op jit(solution)/shard_map/ppermute | solution.py:379
  51.9 1.9 %collective-permute-start.11 = (bf16[128,2048]{1,0:T(8,128)(2,1)}, bf16[128,2048]{1,0:T(8,128)(2,1)S(1)}, u32[]{:S(2)}, u32[]{:S(2)}) collective-permute-start(bf16[128,2048]{1,0:T(8,128)(2,1)} %get-tuple-element.58), channel_id=1, source_target_pairs={{0,16},{4,20},{8,24},{12,28},{16,0},{20,4},{24,8},{28,12},{1,17},{... | collective-permute-start | bytes 1572872 | tf_op jit(solution)/shard_map/ppermute | solution.py:379
  57.5 2.5 %kv_shares.1 = (f32[32,1024]{1,0:T(8,128)S(1)}, f32[32,1024]{1,0:T(8,128)S(1)}, f32[32,1024]{1,0:T(8,128)S(1)}, f32[32,1024]{1,0:T(8,128)S(1)}) custom-call(s32[3]{0:T(128)S(1)} %copy-done.4, bf16[16,1024]{1,0:T(8,128)(2,1)S(1)} %copy-done.6, bf16[16,1024]{1,0:T(8,128)(2,1)S(1)} %collective-permute-done.refs_1_, ...), custom_call_target="tpu_custom_call" | custom-call | flops 536870912 | bytes 4194304 | tf_op jit(solution)/shard_map/kv_shares/pallas_call | solution.py:122
  60.2 1.5 %collective-permute-start.9 = (f32[32,1024]{1,0:T(8,128)S(1)}, f32[32,1024]{1,0:T(8,128)S(1)}, u32[]{:S(2)}, u32[]{:S(2)}) collective-permute-start(f32[32,1024]{1,0:T(8,128)S(1)} %get-tuple-element.56), channel_id=1, source_target_pairs={{0,24},{4,28},{8,16},{12,20},{16,8},{20,12},{24,0},{28,4},{1,25},{... | collective-permute-start | bytes 393224 | tf_op jit(solution)/shard_map/ppermute | solution.py:379
  61.9 1.9 %collective-permute-start.16 = (f32[32,1024]{1,0:T(8,128)S(1)}, f32[32,1024]{1,0:T(8,128)S(1)}, u32[]{:S(2)}, u32[]{:S(2)}) collective-permute-start(f32[32,1024]{1,0:T(8,128)S(1)} %get-tuple-element.65), channel_id=1, source_target_pairs={{0,16},{4,20},{8,24},{12,28},{16,0},{20,4},{24,8},{28,12},{1,17},{... | collective-permute-start | bytes 393224 | tf_op jit(solution)/shard_map/ppermute | solution.py:379
  64.9 4.8 %collective-permute-done.11.own = bf16[128,2048]{1,0:T(8,128)(2,1)S(1)} collective-permute-done((bf16[128,2048]{1,0:T(8,128)(2,1)}, bf16[128,2048]{1,0:T(8,128)(2,1)S(1)}, u32[]{:S(2)}, u32[]{:S(2)}) %collective-permute-start.11) | collective-permute-done | bytes 524320 | tf_op jit(solution)/shard_map/ppermute | solution.py:379
  70.3 1.8 %collective-permute-start.14 = (bf16[512,512]{1,0:T(8,128)(2,1)S(1)}, bf16[512,512]{1,0:T(8,128)(2,1)S(1)}, u32[]{:S(2)}, u32[]{:S(2)}) collective-permute-start(bf16[512,512]{1,0:T(8,128)(2,1)S(1)} %collective-permute-done.13.q_other), channel_id=1, source_target_pairs={{0,8},{4,12},{8,0},{12,4},{16,24},{20,28},{24,16},{28,20},{1,9},{5... | collective-permute-start | bytes 1572872 | tf_op jit(solution)/shard_map/ppermute | solution.py:379
  72.7 1.6 %collective-permute-start.17 = (bf16[512,512]{1,0:T(8,128)(2,1)S(1)}, bf16[512,512]{1,0:T(8,128)(2,1)S(1)}, u32[]{:S(2)}, u32[]{:S(2)}) collective-permute-start(bf16[512,512]{1,0:T(8,128)(2,1)S(1)} %get-tuple-element.68), channel_id=1, source_target_pairs={{0,16},{4,20},{8,24},{12,28},{16,0},{20,4},{24,8},{28,12},{1,17},{... | collective-permute-start | bytes 1572872 | tf_op jit(solution)/shard_map/ppermute | solution.py:379
  74.3 1.6 %collective-permute-start.18 = (bf16[64,256]{1,0:T(8,128)(2,1)S(1)}, bf16[64,256]{1,0:T(8,128)(2,1)S(1)}, u32[]{:S(2)}, u32[]{:S(2)}) collective-permute-start(bf16[64,256]{1,0:T(8,128)(2,1)S(1)} %get-tuple-element.70), channel_id=1, source_target_pairs={{0,1},{1,0},{2,3},{3,2},{4,5},{5,4},{6,7},{7,6},{8,9},{9,8},{10,11... | collective-permute-start | bytes 98312 | tf_op jit(solution)/shard_map/ppermute | solution.py:388
  77.1 1.3 collective-permute-done.18.landed
  78.3 2.6 %collective-permute-start.20 = (bf16[64,256]{1,0:T(8,128)(2,1)S(1)}, bf16[64,256]{1,0:T(8,128)(2,1)S(1)}, u32[]{:S(2)}, u32[]{:S(2)}) collective-permute-start(bf16[64,256]{1,0:T(8,128)(2,1)S(1)} %kv_turn.1), channel_id=1, source_target_pairs={{0,2},{1,3},{2,0},{3,1},{4,6},{5,7},{6,4},{7,5},{8,10},{9,11},{10,... | collective-permute-start | bytes 98312 | tf_op jit(solution)/shard_map/ppermute | solution.py:388
  81.1 3.2 %collective-permute-done.14.q_corner = bf16[512,512]{1,0:T(8,128)(2,1)S(1)} collective-permute-done((bf16[512,512]{1,0:T(8,128)(2,1)S(1)}, bf16[512,512]{1,0:T(8,128)(2,1)S(1)}, u32[]{:S(2)}, u32[]{:S(2)}) %collective-permute-start.14) | collective-permute-done | bytes 524320 | tf_op jit(solution)/shard_map/ppermute | solution.py:379
  84.2 2.2 %collective-permute-done.17.o_early = bf16[512,512]{1,0:T(8,128)(2,1)S(1)} collective-permute-done((bf16[512,512]{1,0:T(8,128)(2,1)S(1)}, bf16[512,512]{1,0:T(8,128)(2,1)S(1)}, u32[]{:S(2)}, u32[]{:S(2)}) %collective-permute-start.17) | collective-permute-done | bytes 524320 | tf_op jit(solution)/shard_map/ppermute | solution.py:379
  87.4 1.6 %collective-permute-start.22 = (bf16[256,512]{1,0:T(8,128)(2,1)S(1)}, bf16[256,512]{1,0:T(8,128)(2,1)S(1)}, u32[]{:S(2)}, u32[]{:S(2)}) collective-permute-start(bf16[256,512]{1,0:T(8,128)(2,1)S(1)} %q_late.3), channel_id=1, source_target_pairs={{0,16},{4,20},{8,24},{12,28},{16,0},{20,4},{24,8},{28,12},{1,17},{... | collective-permute-start | bytes 786440 | tf_op jit(solution)/shard_map/ppermute | solution.py:379
  89.9 2.6 %collective-permute-start.24 = (bf16[128,256]{1,0:T(8,128)(2,1)S(1)}, bf16[128,256]{1,0:T(8,128)(2,1)S(1)}, u32[]{:S(2)}, u32[]{:S(2)}) collective-permute-start(bf16[128,256]{1,0:T(8,128)(2,1)S(1)} %kv_join.1.refs_0_), channel_id=1, source_target_pairs={{0,24},{4,28},{8,16},{12,20},{16,8},{20,12},{24,0},{28,4},{1,25},{... | collective-permute-start | bytes 196616 | tf_op jit(solution)/shard_map/ppermute | solution.py:379
  95.2 4.3 %collective-permute-done.23.refs_2_ = bf16[128,256]{1,0:T(8,128)(2,1)S(1)} collective-permute-done((bf16[128,256]{1,0:T(8,128)(2,1)S(1)}, bf16[128,256]{1,0:T(8,128)(2,1)S(1)}, u32[]{:S(2)}, u32[]{:S(2)}) %collective-permute-start.23) | collective-permute-done | bytes 65568 | tf_op jit(solution)/shard_map/ppermute | solution.py:379
  99.5 2.3 %attend.1.near = bf16[256,512]{1,0:T(8,128)(2,1)S(1)} custom-call(f32[1,128]{1,0:T(1,128)S(1)} %bitcast.10, f32[256,512]{1,0:T(8,128)S(1)} %q_late.2.first, bf16[256,512]{1,0:T(8,128)(2,1)S(1)} %collective-permute-done.22.landed, bf16[128,256]{1,0:T(8,128)(2,1)S(1)} %kv_join.1.refs_0_, bf16[128,256]{1,0:T(8,128)(2,1)S(1)} %collective-permute-done.21.refs_1_, ...), custom_call_target="tpu_custom_call" | custom-call | flops 268435456 | bytes 2097152 | tf_op jit(solution)/shard_map/attend/pallas_call | solution.py:122
  102.2 6.1 %collective-permute-done.28.near = bf16[256,512]{1,0:T(8,128)(2,1)S(1)} collective-permute-done((bf16[256,512]{1,0:T(8,128)(2,1)S(1)}, bf16[256,512]{1,0:T(8,128)(2,1)S(1)}, u32[]{:S(2)}, u32[]{:S(2)}) %collective-permute-start.28) | collective-permute-done | bytes 262176 | tf_op jit(solution)/shard_map/ppermute | solution.py:379
  109.8 1.2 o_share.3
  111.5 1.7 %collective-permute-start.35 = (bf16[128,1024]{1,0:T(8,128)(2,1)S(1)}, bf16[128,1024]{1,0:T(8,128)(2,1)S(1)}, u32[]{:S(2)}, u32[]{:S(2)}) collective-permute-start(bf16[128,1024]{1,0:T(8,128)(2,1)S(1)} %get-tuple-element.86), channel_id=1, source_target_pairs={{0,8},{4,12},{8,0},{12,4},{16,24},{20,28},{24,16},{28,20},{1,9},{5... | collective-permute-start | bytes 786440 | tf_op jit(solution)/shard_map/ppermute | solution.py:379
  113.2 1.2 o_share.2
  114.5 5.9 %collective-permute-done.30.landed = bf16[128,1024]{1,0:T(8,128)(2,1)S(1)} collective-permute-done((bf16[128,1024]{1,0:T(8,128)(2,1)S(1)}, bf16[128,1024]{1,0:T(8,128)(2,1)S(1)}, u32[]{:S(2)}, u32[]{:S(2)}) %collective-permute-start.30) | collective-permute-done | bytes 262176 | tf_op jit(solution)/shard_map/ppermute | solution.py:379
  121.0 1.6 %collective-permute-start.31 = (bf16[128,512]{1,0:T(8,128)(2,1)S(1)}, bf16[128,512]{1,0:T(8,128)(2,1)S(1)}, u32[]{:S(2)}, u32[]{:S(2)}) collective-permute-start(bf16[128,512]{1,0:T(8,128)(2,1)S(1)} %get-tuple-element.82), channel_id=1, source_target_pairs={{0,1},{1,0},{2,3},{3,2},{4,5},{5,4},{6,7},{7,6},{8,9},{9,8},{10,11... | collective-permute-start | bytes 393224 | tf_op jit(solution)/shard_map/ppermute | solution.py:388
  122.6 2.6 %collective-permute-start.32 = (bf16[128,512]{1,0:T(8,128)(2,1)S(1)}, bf16[128,512]{1,0:T(8,128)(2,1)S(1)}, u32[]{:S(2)}, u32[]{:S(2)}) collective-permute-start(bf16[128,512]{1,0:T(8,128)(2,1)S(1)} %get-tuple-element.83), channel_id=1, source_target_pairs={{0,2},{1,3},{2,0},{3,1},{4,6},{5,7},{6,4},{7,5},{8,10},{9,11},{10,... | collective-permute-start | bytes 393224 | tf_op jit(solution)/shard_map/ppermute | solution.py:388
  127.5 3.5 %collective-permute-start.37 = (bf16[128,512]{1,0:T(8,128)(2,1)S(1)}, bf16[128,512]{1,0:T(8,128)(2,1)S(1)}, u32[]{:S(2)}, u32[]{:S(2)}) collective-permute-start(bf16[128,512]{1,0:T(8,128)(2,1)S(1)} %get-tuple-element.89), channel_id=1, source_target_pairs={{0,2},{1,3},{2,0},{3,1},{4,6},{5,7},{6,4},{7,5},{8,10},{9,11},{10,... | collective-permute-start | bytes 393224 | tf_op jit(solution)/shard_map/ppermute | solution.py:388
  131.2 4.2 %collective-permute-done.32.refs_2_ = bf16[128,512]{1,0:T(8,128)(2,1)S(1)} collective-permute-done((bf16[128,512]{1,0:T(8,128)(2,1)S(1)}, bf16[128,512]{1,0:T(8,128)(2,1)S(1)}, u32[]{:S(2)}, u32[]{:S(2)}) %collective-permute-start.32) | collective-permute-done | bytes 131104 | tf_op jit(solution)/shard_map/ppermute | solution.py:388
  135.6 9.8 %collective-permute-done.37.refs_2_ = bf16[128,512]{1,0:T(8,128)(2,1)S(1)} collective-permute-done((bf16[128,512]{1,0:T(8,128)(2,1)S(1)}, bf16[128,512]{1,0:T(8,128)(2,1)S(1)}, u32[]{:S(2)}, u32[]{:S(2)}) %collective-permute-start.37) | collective-permute-done | bytes 131104 | tf_op jit(solution)/shard_map/ppermute | solution.py:388
  145.3 1.3 mix_keep.1
  (96 shorter events, 18.0 us)
Async XLA Ops:
  0.0 56.6 %collective-permute-start.7 = (bf16[512,2048]{1,0:T(8,128)(2,1)}, bf16[512,2048]{1,0:T(8,128)(2,1)}, u32[]{:S(2)}, u32[]{:S(2)}) collective-permute-start(bf16[512,2048]{1,0:T(8,128)(2,1)} %refs_8_.1), channel_id=1, source_target_pairs={{0,4},{4,0},{8,12},{12,8},{16,20},{20,16},{24,28},{28,24},{1,5},{5... | collective-permute-start | bytes 6291464 | tf_op jit(solution)/shard_map/ppermute | solution.py:376
  35.7 26.3 %collective-permute-start.10 = (bf16[512,512]{1,0:T(8,128)(2,1)}, bf16[512,512]{1,0:T(8,128)(2,1)S(1)}, u32[]{:S(2)}, u32[]{:S(2)}) collective-permute-start(bf16[512,512]{1,0:T(8,128)(2,1)} %get-tuple-element.57.q_keep), channel_id=1, source_target_pairs={{0,8},{4,12},{8,0},{12,4},{16,24},{20,28},{24,16},{28,20},{1,9},{5... | collective-permute-start | bytes 1572872 | tf_op jit(solution)/shard_map/ppermute | solution.py:379
  38.2 13.7 %collective-permute-start = (bf16[16,1024]{1,0:T(8,128)(2,1)}, bf16[16,1024]{1,0:T(8,128)(2,1)S(1)}, u32[]{:S(2)}, u32[]{:S(2)}) collective-permute-start(bf16[16,1024]{1,0:T(8,128)(2,1)} %get-tuple-element.49), channel_id=1, source_target_pairs={{0,8},{4,12},{8,0},{12,4},{16,24},{20,28},{24,16},{28,20},{1,9},{5... | collective-permute-start | bytes 98312 | tf_op jit(solution)/shard_map/ppermute | solution.py:379
  38.3 15.6 %collective-permute-start.1 = (bf16[16,1024]{1,0:T(8,128)(2,1)}, bf16[16,1024]{1,0:T(8,128)(2,1)S(1)}, u32[]{:S(2)}, u32[]{:S(2)}) collective-permute-start(bf16[16,1024]{1,0:T(8,128)(2,1)} %get-tuple-element.50), channel_id=1, source_target_pairs={{0,16},{4,20},{8,24},{12,28},{16,0},{20,4},{24,8},{28,12},{1,17},{... | collective-permute-start | bytes 98312 | tf_op jit(solution)/shard_map/ppermute | solution.py:379
  40.3 13.6 %collective-permute-start.2 = (bf16[16,1024]{1,0:T(8,128)(2,1)}, bf16[16,1024]{1,0:T(8,128)(2,1)S(1)}, u32[]{:S(2)}, u32[]{:S(2)}) collective-permute-start(bf16[16,1024]{1,0:T(8,128)(2,1)} %get-tuple-element.51), channel_id=1, source_target_pairs={{0,24},{4,28},{8,16},{12,20},{16,8},{20,12},{24,0},{28,4},{1,25},{... | collective-permute-start | bytes 98312 | tf_op jit(solution)/shard_map/ppermute | solution.py:379
  51.9 17.8 %collective-permute-start.11 = (bf16[128,2048]{1,0:T(8,128)(2,1)}, bf16[128,2048]{1,0:T(8,128)(2,1)S(1)}, u32[]{:S(2)}, u32[]{:S(2)}) collective-permute-start(bf16[128,2048]{1,0:T(8,128)(2,1)} %get-tuple-element.58), channel_id=1, source_target_pairs={{0,16},{4,20},{8,24},{12,28},{16,0},{20,4},{24,8},{28,12},{1,17},{... | collective-permute-start | bytes 1572872 | tf_op jit(solution)/shard_map/ppermute | solution.py:379
  56.5 13.8 %collective-permute-start.13 = (bf16[512,512]{1,0:T(8,128)(2,1)}, bf16[512,512]{1,0:T(8,128)(2,1)S(1)}, u32[]{:S(2)}, u32[]{:S(2)}) collective-permute-start(bf16[512,512]{1,0:T(8,128)(2,1)} %get-tuple-element.62), channel_id=1, source_target_pairs={{0,4},{4,0},{8,12},{12,8},{16,20},{20,16},{24,28},{28,24},{1,5},{5... | collective-permute-start | bytes 1572872 | tf_op jit(solution)/shard_map/ppermute | solution.py:376
  60.2 9.6 %collective-permute-start.9 = (f32[32,1024]{1,0:T(8,128)S(1)}, f32[32,1024]{1,0:T(8,128)S(1)}, u32[]{:S(2)}, u32[]{:S(2)}) collective-permute-start(f32[32,1024]{1,0:T(8,128)S(1)} %get-tuple-element.56), channel_id=1, source_target_pairs={{0,24},{4,28},{8,16},{12,20},{16,8},{20,12},{24,0},{28,4},{1,25},{... | collective-permute-start | bytes 393224 | tf_op jit(solution)/shard_map/ppermute | solution.py:379
  61.7 10.3 %collective-permute-start.15 = (f32[32,1024]{1,0:T(8,128)S(1)}, f32[32,1024]{1,0:T(8,128)S(1)}, u32[]{:S(2)}, u32[]{:S(2)}) collective-permute-start(f32[32,1024]{1,0:T(8,128)S(1)} %get-tuple-element.64), channel_id=1, source_target_pairs={{0,8},{4,12},{8,0},{12,4},{16,24},{20,28},{24,16},{28,20},{1,9},{5... | collective-permute-start | bytes 393224 | tf_op jit(solution)/shard_map/ppermute | solution.py:379
  61.9 10.2 %collective-permute-start.16 = (f32[32,1024]{1,0:T(8,128)S(1)}, f32[32,1024]{1,0:T(8,128)S(1)}, u32[]{:S(2)}, u32[]{:S(2)}) collective-permute-start(f32[32,1024]{1,0:T(8,128)S(1)} %get-tuple-element.65), channel_id=1, source_target_pairs={{0,16},{4,20},{8,24},{12,28},{16,0},{20,4},{24,8},{28,12},{1,17},{... | collective-permute-start | bytes 393224 | tf_op jit(solution)/shard_map/ppermute | solution.py:379
  69.8 6.3 %collective-permute-start.19 = (bf16[128,2048]{1,0:T(8,128)(2,1)S(1)}, bf16[128,2048]{1,0:T(8,128)(2,1)S(1)}, u32[]{:S(2)}, u32[]{:S(2)}) collective-permute-start(bf16[128,2048]{1,0:T(8,128)(2,1)S(1)} %collective-permute-done.11.own), channel_id=1, source_target_pairs={{0,4},{4,0},{8,12},{12,8},{16,20},{20,16},{24,28},{28,24},{1,5},{5... | collective-permute-start | bytes 1572872 | tf_op jit(solution)/shard_map/ppermute | solution.py:376
  70.3 14.0 %collective-permute-start.14 = (bf16[512,512]{1,0:T(8,128)(2,1)S(1)}, bf16[512,512]{1,0:T(8,128)(2,1)S(1)}, u32[]{:S(2)}, u32[]{:S(2)}) collective-permute-start(bf16[512,512]{1,0:T(8,128)(2,1)S(1)} %collective-permute-done.13.q_other), channel_id=1, source_target_pairs={{0,8},{4,12},{8,0},{12,4},{16,24},{20,28},{24,16},{28,20},{1,9},{5... | collective-permute-start | bytes 1572872 | tf_op jit(solution)/shard_map/ppermute | solution.py:379
  72.7 13.7 %collective-permute-start.17 = (bf16[512,512]{1,0:T(8,128)(2,1)S(1)}, bf16[512,512]{1,0:T(8,128)(2,1)S(1)}, u32[]{:S(2)}, u32[]{:S(2)}) collective-permute-start(bf16[512,512]{1,0:T(8,128)(2,1)S(1)} %get-tuple-element.68), channel_id=1, source_target_pairs={{0,16},{4,20},{8,24},{12,28},{16,0},{20,4},{24,8},{28,12},{1,17},{... | collective-permute-start | bytes 1572872 | tf_op jit(solution)/shard_map/ppermute | solution.py:379
  76.0 16.6 %collective-permute-start.12 = (bf16[128,2048]{1,0:T(8,128)(2,1)S(1)}, bf16[128,2048]{1,0:T(8,128)(2,1)S(1)}, u32[]{:S(2)}, u32[]{:S(2)}) collective-permute-start(bf16[128,2048]{1,0:T(8,128)(2,1)S(1)} %get-tuple-element.60.own), channel_id=1, source_target_pairs={{0,4},{4,0},{8,12},{12,8},{16,20},{20,16},{24,28},{28,24},{1,5},{5... | collective-permute-start | bytes 1572872 | tf_op jit(solution)/shard_map/ppermute | solution.py:376
  78.3 10.7 %collective-permute-start.20 = (bf16[64,256]{1,0:T(8,128)(2,1)S(1)}, bf16[64,256]{1,0:T(8,128)(2,1)S(1)}, u32[]{:S(2)}, u32[]{:S(2)}) collective-permute-start(bf16[64,256]{1,0:T(8,128)(2,1)S(1)} %kv_turn.1), channel_id=1, source_target_pairs={{0,2},{1,3},{2,0},{3,1},{4,6},{5,7},{6,4},{7,5},{8,10},{9,11},{10,... | collective-permute-start | bytes 98312 | tf_op jit(solution)/shard_map/ppermute | solution.py:388
  87.4 12.1 %collective-permute-start.22 = (bf16[256,512]{1,0:T(8,128)(2,1)S(1)}, bf16[256,512]{1,0:T(8,128)(2,1)S(1)}, u32[]{:S(2)}, u32[]{:S(2)}) collective-permute-start(bf16[256,512]{1,0:T(8,128)(2,1)S(1)} %q_late.3), channel_id=1, source_target_pairs={{0,16},{4,20},{8,24},{12,28},{16,0},{20,4},{24,8},{28,12},{1,17},{... | collective-permute-start | bytes 786440 | tf_op jit(solution)/shard_map/ppermute | solution.py:379
  89.0 5.2 %collective-permute-start.21 = (bf16[128,256]{1,0:T(8,128)(2,1)S(1)}, bf16[128,256]{1,0:T(8,128)(2,1)S(1)}, u32[]{:S(2)}, u32[]{:S(2)}) collective-permute-start(bf16[128,256]{1,0:T(8,128)(2,1)S(1)} %kv_join.1.refs_0_), channel_id=1, source_target_pairs={{0,8},{4,12},{8,0},{12,4},{16,24},{20,28},{24,16},{28,20},{1,9},{5... | collective-permute-start | bytes 196616 | tf_op jit(solution)/shard_map/ppermute | solution.py:379
  89.6 9.9 %collective-permute-start.23 = (bf16[128,256]{1,0:T(8,128)(2,1)S(1)}, bf16[128,256]{1,0:T(8,128)(2,1)S(1)}, u32[]{:S(2)}, u32[]{:S(2)}) collective-permute-start(bf16[128,256]{1,0:T(8,128)(2,1)S(1)} %kv_join.1.refs_0_), channel_id=1, source_target_pairs={{0,16},{4,20},{8,24},{12,28},{16,0},{20,4},{24,8},{28,12},{1,17},{... | collective-permute-start | bytes 196616 | tf_op jit(solution)/shard_map/ppermute | solution.py:379
  89.9 9.6 %collective-permute-start.24 = (bf16[128,256]{1,0:T(8,128)(2,1)S(1)}, bf16[128,256]{1,0:T(8,128)(2,1)S(1)}, u32[]{:S(2)}, u32[]{:S(2)}) collective-permute-start(bf16[128,256]{1,0:T(8,128)(2,1)S(1)} %kv_join.1.refs_0_), channel_id=1, source_target_pairs={{0,24},{4,28},{8,16},{12,20},{16,8},{20,12},{24,0},{28,4},{1,25},{... | collective-permute-start | bytes 196616 | tf_op jit(solution)/shard_map/ppermute | solution.py:379
  92.6 16.2 %collective-permute-start.27 = (bf16[512,512]{1,0:T(8,128)(2,1)S(1)}, bf16[512,512]{1,0:T(8,128)(2,1)S(1)}, u32[]{:S(2)}, u32[]{:S(2)}) collective-permute-start(bf16[512,512]{1,0:T(8,128)(2,1)S(1)} %get-tuple-element.78), channel_id=1, source_target_pairs={{0,16},{4,20},{8,24},{12,28},{16,0},{20,4},{24,8},{28,12},{1,17},{... | collective-permute-start | bytes 1572872 | tf_op jit(solution)/shard_map/ppermute | solution.py:379
  101.9 6.4 %collective-permute-start.28 = (bf16[256,512]{1,0:T(8,128)(2,1)S(1)}, bf16[256,512]{1,0:T(8,128)(2,1)S(1)}, u32[]{:S(2)}, u32[]{:S(2)}) collective-permute-start(bf16[256,512]{1,0:T(8,128)(2,1)S(1)} %attend.1.near), channel_id=1, source_target_pairs={{0,8},{4,12},{8,0},{12,4},{16,24},{20,28},{24,16},{28,20},{1,9},{5... | collective-permute-start | bytes 786440 | tf_op jit(solution)/shard_map/ppermute | solution.py:379
  108.3 4.9 %collective-permute-start.26 = (bf16[256,512]{1,0:T(8,128)(2,1)S(1)}, bf16[256,512]{1,0:T(8,128)(2,1)S(1)}, u32[]{:S(2)}, u32[]{:S(2)}) collective-permute-start(bf16[256,512]{1,0:T(8,128)(2,1)S(1)} %attend.1.near), channel_id=1, source_target_pairs={{0,4},{4,0},{8,12},{12,8},{16,20},{20,16},{24,28},{28,24},{1,5},{5... | collective-permute-start | bytes 786440 | tf_op jit(solution)/shard_map/ppermute | solution.py:376
  111.1 9.2 %collective-permute-start.30 = (bf16[128,1024]{1,0:T(8,128)(2,1)S(1)}, bf16[128,1024]{1,0:T(8,128)(2,1)S(1)}, u32[]{:S(2)}, u32[]{:S(2)}) collective-permute-start(bf16[128,1024]{1,0:T(8,128)(2,1)S(1)} %get-tuple-element.80), channel_id=1, source_target_pairs={{0,8},{4,12},{8,0},{12,4},{16,24},{20,28},{24,16},{28,20},{1,9},{5... | collective-permute-start | bytes 786440 | tf_op jit(solution)/shard_map/ppermute | solution.py:379
  111.5 14.6 %collective-permute-start.35 = (bf16[128,1024]{1,0:T(8,128)(2,1)S(1)}, bf16[128,1024]{1,0:T(8,128)(2,1)S(1)}, u32[]{:S(2)}, u32[]{:S(2)}) collective-permute-start(bf16[128,1024]{1,0:T(8,128)(2,1)S(1)} %get-tuple-element.86), channel_id=1, source_target_pairs={{0,8},{4,12},{8,0},{12,4},{16,24},{20,28},{24,16},{28,20},{1,9},{5... | collective-permute-start | bytes 786440 | tf_op jit(solution)/shard_map/ppermute | solution.py:379
  113.2 14.3 %collective-permute-start.8 = (bf16[128,512]{1,0:T(8,128)(2,1)S(1)}, bf16[128,512]{1,0:T(8,128)(2,1)S(1)}, u32[]{:S(2)}, u32[]{:S(2)}) collective-permute-start(bf16[128,512]{1,0:T(8,128)(2,1)S(1)} %get-tuple-element.55), channel_id=1, source_target_pairs={{0,4},{4,0},{8,12},{12,8},{16,20},{20,16},{24,28},{28,24},{1,5},{5... | collective-permute-start | bytes 393224 | tf_op jit(solution)/shard_map/ppermute | solution.py:376
  121.0 10.1 %collective-permute-start.31 = (bf16[128,512]{1,0:T(8,128)(2,1)S(1)}, bf16[128,512]{1,0:T(8,128)(2,1)S(1)}, u32[]{:S(2)}, u32[]{:S(2)}) collective-permute-start(bf16[128,512]{1,0:T(8,128)(2,1)S(1)} %get-tuple-element.82), channel_id=1, source_target_pairs={{0,1},{1,0},{2,3},{3,2},{4,5},{5,4},{6,7},{7,6},{8,9},{9,8},{10,11... | collective-permute-start | bytes 393224 | tf_op jit(solution)/shard_map/ppermute | solution.py:388
  122.6 12.8 %collective-permute-start.32 = (bf16[128,512]{1,0:T(8,128)(2,1)S(1)}, bf16[128,512]{1,0:T(8,128)(2,1)S(1)}, u32[]{:S(2)}, u32[]{:S(2)}) collective-permute-start(bf16[128,512]{1,0:T(8,128)(2,1)S(1)} %get-tuple-element.83), channel_id=1, source_target_pairs={{0,2},{1,3},{2,0},{3,1},{4,6},{5,7},{6,4},{7,5},{8,10},{9,11},{10,... | collective-permute-start | bytes 393224 | tf_op jit(solution)/shard_map/ppermute | solution.py:388
  125.2 10.2 %collective-permute-start.33 = (bf16[128,512]{1,0:T(8,128)(2,1)S(1)}, bf16[128,512]{1,0:T(8,128)(2,1)S(1)}, u32[]{:S(2)}, u32[]{:S(2)}) collective-permute-start(bf16[128,512]{1,0:T(8,128)(2,1)S(1)} %get-tuple-element.84), channel_id=1, source_target_pairs={{0,3},{1,2},{2,1},{3,0},{4,7},{5,6},{6,5},{7,4},{8,11},{9,10},{10,... | collective-permute-start | bytes 393224 | tf_op jit(solution)/shard_map/ppermute | solution.py:388
  126.8 8.8 %collective-permute-start.36 = (bf16[128,512]{1,0:T(8,128)(2,1)S(1)}, bf16[128,512]{1,0:T(8,128)(2,1)S(1)}, u32[]{:S(2)}, u32[]{:S(2)}) collective-permute-start(bf16[128,512]{1,0:T(8,128)(2,1)S(1)} %get-tuple-element.88), channel_id=1, source_target_pairs={{0,1},{1,0},{2,3},{3,2},{4,5},{5,4},{6,7},{7,6},{8,9},{9,8},{10,11... | collective-permute-start | bytes 393224 | tf_op jit(solution)/shard_map/ppermute | solution.py:388
  127.5 17.8 %collective-permute-start.37 = (bf16[128,512]{1,0:T(8,128)(2,1)S(1)}, bf16[128,512]{1,0:T(8,128)(2,1)S(1)}, u32[]{:S(2)}, u32[]{:S(2)}) collective-permute-start(bf16[128,512]{1,0:T(8,128)(2,1)S(1)} %get-tuple-element.89), channel_id=1, source_target_pairs={{0,2},{1,3},{2,0},{3,1},{4,6},{5,7},{6,4},{7,5},{8,10},{9,11},{10,... | collective-permute-start | bytes 393224 | tf_op jit(solution)/shard_map/ppermute | solution.py:388
  131.0 14.3 %collective-permute-start.38 = (bf16[128,512]{1,0:T(8,128)(2,1)S(1)}, bf16[128,512]{1,0:T(8,128)(2,1)S(1)}, u32[]{:S(2)}, u32[]{:S(2)}) collective-permute-start(bf16[128,512]{1,0:T(8,128)(2,1)S(1)} %get-tuple-element.90), channel_id=1, source_target_pairs={{0,3},{1,2},{2,1},{3,0},{4,7},{5,6},{6,5},{7,4},{8,11},{9,10},{10,... | collective-permute-start | bytes 393224 | tf_op jit(solution)/shard_map/ppermute | solution.py:388
  135.5 9.9 %collective-permute-start.34 = (bf16[128,512]{1,0:T(8,128)(2,1)S(1)}, bf16[128,512]{1,0:T(8,128)(2,1)S(1)}, u32[]{:S(2)}, u32[]{:S(2)}) collective-permute-start(bf16[128,512]{1,0:T(8,128)(2,1)S(1)} %mix_give.1), channel_id=1, source_target_pairs={{0,4},{4,0},{8,12},{12,8},{16,20},{20,16},{24,28},{28,24},{1,5},{5... | collective-permute-start | bytes 393224 | tf_op jit(solution)/shard_map/ppermute | solution.py:376
  (19 other events, 191.8 us)
where the time goes:
time: 147 us
  waiting for transfers between devices  54.5 us (37%)
  Pallas kernels  50.1 us (34%)
  starting transfers between devices  39 us (27%)
    pallas_call x17, Pallas kernels, call(): pl.pallas_call(kernel, out_shape=outs, in_specs=specs, out_specs=[VMEM] *...  50.1 us
    ppermute x18, waiting for transfers between devices, peer(): return lax.ppermute(x, 'ctx', [(k, k ^ 2 * s) for k in range(ctx_count)])  36.7 us
    ppermute x18, starting transfers between devices, peer(): return lax.ppermute(x, 'ctx', [(k, k ^ 2 * s) for k in range(ctx_count)])  23.1 us
    ppermute x8, waiting for transfers between devices, across(): return lax.ppermute(x, 'img', [(k, k ^ t) for k in range(CHIPS)])  15.2 us
    ppermute x8, starting transfers between devices, across(): return lax.ppermute(x, 'img', [(k, k ^ t) for k in range(CHIPS)])  13.1 us
  transfers between devices with their start and end apart: 39, of which 13 were waited for; matrix products, arithmetic and copies ran while one was open for 1% of the time, Pallas kernels for 33%

commit v1 on v0

--- a/solution.py
+++ b/solution.py
@@ -399,7 +399,6 @@
         [shape(vis_here, part)] * CHIPS
         + [shape(tokens, width // 2)]
         + [shape(rows_dev, half)] * 2,
-        out_specs=[VMEM] * (1 + CHIPS) + [anywhere] * 2,
         scratch=[
             pltpu.VMEM((tokens, width), BF16),
             pltpu.VMEM((vis_here, width), BF16),
@@ -413,7 +412,8 @@
     )
     vis_own = [vis_pieces[0]] + [peer(vis_pieces[s], s) for s in steps]
     vis_other = [swap(x) for x in vis_own]
-    q_side, q_other = along_x(q_keep), swap(q_give)
+    q_keep_sent, far, _ = lax.optimization_barrier((q_keep, far, vis_own))
+    q_side, q_other = along_x(q_keep_sent), swap(q_give)
     far = along_y(far)
 
     shares = call(
@@ -442,7 +442,7 @@
         name="near",
     )
     shares = [shares[0]] + [peer(shares[s], s) for s in steps]
-    shares[3], q_side, far, near = lax.optimization_barrier((shares[3], q_side, far, near))
+    shares, q_side, far, near = lax.optimization_barrier((shares, q_side, far, near))
     here, there, give = call(
         kv_norm_kernel,
         (where, k_gain[None], *shares),
@@ -485,8 +485,8 @@
     q_corner = along_x(q_behind)
 
     o_early, _ = lax.optimization_barrier((o_weight[:half], here))
-    q_corner, o_early = lax.optimization_barrier((q_corner, along_y(o_early)))
-    early[1], kv_all[1] = lax.optimization_barrier((early[1], kv_all[1]))
+    o_early = along_y(o_early)
+    early[1], o_early = lax.optimization_barrier((early[1], o_early))
     q_far, q_first = [
         call(
             late_kernel,
@@ -499,8 +499,9 @@
         )[0]
         for k, kind in ((0, BF16), (1, F32))
     ]
-    landed = along_y(q_far)
-    o_late, _ = lax.optimization_barrier((o_weight[half:], q_far))
+    q_sent, kv_all[2] = lax.optimization_barrier((q_far, kv_all[2]))
+    landed = along_y(q_sent)
+    o_late, _ = lax.optimization_barrier((o_weight[half:], q_sent))
     o_late = along_y(o_late)
 
     ids = jnp.concatenate((segment_ids, swap(segment_ids)))

time: 147 us -> 109 us (0.74)
  Pallas kernels: 50.1 us -> 19.7 us
  starting transfers between devices: 39 us -> 32.7 us
    pallas_call x17, Pallas kernels: 50.1 us -> 19.7 us  [call(): pl.pallas_call(kernel, out_shape=outs, in_specs=specs, out_specs=[VMEM] *...]
    ppermute x18, starting transfers between devices: 23.1 us -> 17.3 us  [peer(): return lax.ppermute(x, 'ctx', [(k, k ^ 2 * s) for k in range(ctx_count)])]
    ppermute x18, waiting for transfers between devices: 36.7 us -> 34.5 us  [peer(): return lax.ppermute(x, 'ctx', [(k, k ^ 2 * s) for k in range(ctx_count)])]
    ppermute x8, waiting for transfers between devices: 15.2 us -> 16.7 us  [across(): return lax.ppermute(x, 'img', [(k, k ^ t) for k in range(CHIPS)])]
  transfers between devices with their start and end apart: 39 -> 39, of which waited for: 13 -> 20; matrix products, arithmetic and copies ran while one was open for 1% -> 1% of each run, Pallas kernels for 33% -> 17%
where the time goes in v1:
time: 109 us
  waiting for transfers between devices  53.1 us (49%)
  starting transfers between devices  32.7 us (30%)
  Pallas kernels  19.7 us (18%)
    ppermute x18, waiting for transfers between devices, peer(): return lax.ppermute(x, 'ctx', [(k, k ^ 2 * s) for k in range(ctx_count)])  34.5 us
    pallas_call x17, Pallas kernels, call(): pl.pallas_call(kernel, out_shape=outs, in_specs=specs, out_specs=[VMEM] *...  19.7 us
    ppermute x18, starting transfers between devices, peer(): return lax.ppermute(x, 'ctx', [(k, k ^ 2 * s) for k in range(ctx_count)])  17.3 us
    ppermute x8, waiting for transfers between devices, across(): return lax.ppermute(x, 'img', [(k, k ^ t) for k in range(CHIPS)])  16.7 us
    ppermute x8, starting transfers between devices, across(): return lax.ppermute(x, 'img', [(k, k ^ t) for k in range(CHIPS)])  13.1 us
    ppermute x13, starting transfers between devices, swap(): return lax.ppermute(x, 'ctx', [(k, k ^ 1) for k in range(ctx_count)])  2.23 us
  transfers between devices with their start and end apart: 39, of which 20 were waited for; matrix products, arithmetic and copies ran while one was open for 1% of the time, Pallas kernels for 17%

profile of v1, /device:TPU:0, one launch (start us, length us, event | category | flops | bytes accessed | tf_op | source)
XLA Modules:
  0.0 108.5 jit_solution(6895595718715042477)
XLA Ops:
  1.1 4.0 %start.1 = (bf16[16,1024]{1,0:T(8,128)(2,1)}, bf16[16,1024]{1,0:T(8,128)(2,1)}, bf16[16,1024]{1,0:T(8,128)(2,1)}, bf16[16,1024]{1,0:T(8,128)(2,1)}, bf16[128,204...) custom-call(s32[3]{0:T(128)} %pad_add_fusion.1.where, bf16[128,4096]{1,0:T(8,128)(2,1)} %text.1, ...), custom_call_target="tpu_custom_call" | custom-call | flops 4194304 | bytes 4194304 | tf_op jit(solution)/shard_map/start/pallas_call | solution.py:122
  5.2 2.6 %collective-permute-start = (bf16[16,1024]{1,0:T(8,128)(2,1)}, bf16[16,1024]{1,0:T(8,128)(2,1)S(1)}, u32[]{:S(2)}, u32[]{:S(2)}) collective-permute-start(bf16[16,1024]{1,0:T(8,128)(2,1)} %get-tuple-element.54), channel_id=1, source_target_pairs={{0,8},{4,12},{8,0},{12,4},{16,24},{20,28},{24,16},{28,20},{1,9},{5... | collective-permute-start | bytes 98312 | tf_op jit(solution)/shard_map/ppermute | solution.py:379
  7.7 1.5 %collective-permute-start.1 = (bf16[16,1024]{1,0:T(8,128)(2,1)}, bf16[16,1024]{1,0:T(8,128)(2,1)S(1)}, u32[]{:S(2)}, u32[]{:S(2)}) collective-permute-start(bf16[16,1024]{1,0:T(8,128)(2,1)} %get-tuple-element.55), channel_id=1, source_target_pairs={{0,16},{4,20},{8,24},{12,28},{16,0},{20,4},{24,8},{28,12},{1,17},{... | collective-permute-start | bytes 98312 | tf_op jit(solution)/shard_map/ppermute | solution.py:379
  10.0 1.9 %collective-permute-done.1.refs_2_ = bf16[16,1024]{1,0:T(8,128)(2,1)S(1)} collective-permute-done((bf16[16,1024]{1,0:T(8,128)(2,1)}, bf16[16,1024]{1,0:T(8,128)(2,1)S(1)}, u32[]{:S(2)}, u32[]{:S(2)}) %collective-permute-start.1) | collective-permute-done | bytes 32800 | tf_op jit(solution)/shard_map/ppermute | solution.py:379
  11.8 2.4 %collective-permute-done.2.refs_3_ = bf16[16,1024]{1,0:T(8,128)(2,1)S(1)} collective-permute-done((bf16[16,1024]{1,0:T(8,128)(2,1)}, bf16[16,1024]{1,0:T(8,128)(2,1)S(1)}, u32[]{:S(2)}, u32[]{:S(2)}) %collective-permute-start.2) | collective-permute-done | bytes 32800 | tf_op jit(solution)/shard_map/ppermute | solution.py:379
  18.5 2.6 %kv_shares.1 = (f32[32,1024]{1,0:T(8,128)S(1)}, f32[32,1024]{1,0:T(8,128)S(1)}, f32[32,1024]{1,0:T(8,128)S(1)}, f32[32,1024]{1,0:T(8,128)S(1)}) custom-call(s32[3]{0:T(128)S(1)} %copy-done.4, bf16[16,1024]{1,0:T(8,128)(2,1)S(1)} %copy-done.6, bf16[16,1024]{1,0:T(8,128)(2,1)S(1)} %collective-permute-done.refs_1_, ...), custom_call_target="tpu_custom_call" | custom-call | flops 536870912 | bytes 4194304 | tf_op jit(solution)/shard_map/kv_shares/pallas_call | solution.py:122
  21.2 2.0 %collective-permute-start.10 = (f32[32,1024]{1,0:T(8,128)S(1)}, f32[32,1024]{1,0:T(8,128)S(1)}, u32[]{:S(2)}, u32[]{:S(2)}) collective-permute-start(f32[32,1024]{1,0:T(8,128)S(1)} %get-tuple-element.62), channel_id=1, source_target_pairs={{0,16},{4,20},{8,24},{12,28},{16,0},{20,4},{24,8},{28,12},{1,17},{... | collective-permute-start | bytes 393224 | tf_op jit(solution)/shard_map/ppermute | solution.py:379
  23.2 1.4 %collective-permute-start.11 = (f32[32,1024]{1,0:T(8,128)S(1)}, f32[32,1024]{1,0:T(8,128)S(1)}, u32[]{:S(2)}, u32[]{:S(2)}) collective-permute-start(f32[32,1024]{1,0:T(8,128)S(1)} %get-tuple-element.63), channel_id=1, source_target_pairs={{0,24},{4,28},{8,16},{12,20},{16,8},{20,12},{24,0},{28,4},{1,25},{... | collective-permute-start | bytes 393224 | tf_op jit(solution)/shard_map/ppermute | solution.py:379
  24.6 3.9 %collective-permute-done.12.q_side = bf16[512,512]{1,0:T(8,128)(2,1)S(1)} collective-permute-done((bf16[512,512]{1,0:T(8,128)(2,1)}, bf16[512,512]{1,0:T(8,128)(2,1)S(1)}, u32[]{:S(2)}, u32[]{:S(2)}) %collective-permute-start.12) | collective-permute-done | bytes 524320 | tf_op jit(solution)/shard_map/ppermute | solution.py:379
  29.6 2.0 %collective-permute-done.13.own = bf16[128,2048]{1,0:T(8,128)(2,1)S(1)} collective-permute-done((bf16[128,2048]{1,0:T(8,128)(2,1)}, bf16[128,2048]{1,0:T(8,128)(2,1)S(1)}, u32[]{:S(2)}, u32[]{:S(2)}) %collective-permute-start.13) | collective-permute-done | bytes 524320 | tf_op jit(solution)/shard_map/ppermute | solution.py:379
  31.6 1.4 %collective-permute-done.10.refs_2_ = f32[32,1024]{1,0:T(8,128)S(1)} collective-permute-done((f32[32,1024]{1,0:T(8,128)S(1)}, f32[32,1024]{1,0:T(8,128)S(1)}, u32[]{:S(2)}, u32[]{:S(2)}) %collective-permute-start.10) | collective-permute-done | bytes 131104 | tf_op jit(solution)/shard_map/ppermute | solution.py:379
  33.6 1.0 collective-permute-start.16
  35.3 1.6 %collective-permute-start.19 = (bf16[64,256]{1,0:T(8,128)(2,1)S(1)}, bf16[64,256]{1,0:T(8,128)(2,1)S(1)}, u32[]{:S(2)}, u32[]{:S(2)}) collective-permute-start(bf16[64,256]{1,0:T(8,128)(2,1)S(1)} %get-tuple-element.81), channel_id=1, source_target_pairs={{0,1},{1,0},{2,3},{3,2},{4,5},{5,4},{6,7},{7,6},{8,9},{9,8},{10,11... | collective-permute-start | bytes 98312 | tf_op jit(solution)/shard_map/ppermute | solution.py:388
  39.3 2.6 %collective-permute-start.20 = (bf16[64,256]{1,0:T(8,128)(2,1)S(1)}, bf16[64,256]{1,0:T(8,128)(2,1)S(1)}, u32[]{:S(2)}, u32[]{:S(2)}) collective-permute-start(bf16[64,256]{1,0:T(8,128)(2,1)S(1)} %kv_turn.1), channel_id=1, source_target_pairs={{0,2},{1,3},{2,0},{3,1},{4,6},{5,7},{6,4},{7,5},{8,10},{9,11},{10,... | collective-permute-start | bytes 98312 | tf_op jit(solution)/shard_map/ppermute | solution.py:388
  42.0 2.1 %collective-permute-done.20.last = bf16[64,256]{1,0:T(8,128)(2,1)S(1)} collective-permute-done((bf16[64,256]{1,0:T(8,128)(2,1)S(1)}, bf16[64,256]{1,0:T(8,128)(2,1)S(1)}, u32[]{:S(2)}, u32[]{:S(2)}) %collective-permute-start.20) | collective-permute-done | bytes 32800 | tf_op jit(solution)/shard_map/ppermute | solution.py:388
  45.3 2.7 %collective-permute-done.16.q_corner = bf16[512,512]{1,0:T(8,128)(2,1)S(1)} collective-permute-done((bf16[512,512]{1,0:T(8,128)(2,1)S(1)}, bf16[512,512]{1,0:T(8,128)(2,1)S(1)}, u32[]{:S(2)}, u32[]{:S(2)}) %collective-permute-start.16) | collective-permute-done | bytes 524320 | tf_op jit(solution)/shard_map/ppermute | solution.py:379
  49.0 1.0 collective-permute-start.23
  50.4 1.8 %collective-permute-done.21.refs_2_ = bf16[128,256]{1,0:T(8,128)(2,1)S(1)} collective-permute-done((bf16[128,256]{1,0:T(8,128)(2,1)S(1)}, bf16[128,256]{1,0:T(8,128)(2,1)S(1)}, u32[]{:S(2)}, u32[]{:S(2)}) %collective-permute-start.21) | collective-permute-done | bytes 65568 | tf_op jit(solution)/shard_map/ppermute | solution.py:379
  54.8 1.6 %collective-permute-start.27 = (bf16[512,512]{1,0:T(8,128)(2,1)S(1)}, bf16[512,512]{1,0:T(8,128)(2,1)S(1)}, u32[]{:S(2)}, u32[]{:S(2)}) collective-permute-start(bf16[512,512]{1,0:T(8,128)(2,1)S(1)} %get-tuple-element.88), channel_id=1, source_target_pairs={{0,16},{4,20},{8,24},{12,28},{16,0},{20,4},{24,8},{28,12},{1,17},{... | collective-permute-start | bytes 1572872 | tf_op jit(solution)/shard_map/ppermute | solution.py:379
  56.4 5.1 %collective-permute-done.22.landed = bf16[256,512]{1,0:T(8,128)(2,1)S(1)} collective-permute-done((bf16[256,512]{1,0:T(8,128)(2,1)S(1)}, bf16[256,512]{1,0:T(8,128)(2,1)S(1)}, u32[]{:S(2)}, u32[]{:S(2)}) %collective-permute-start.22) | collective-permute-done | bytes 262176 | tf_op jit(solution)/shard_map/ppermute | solution.py:379
  61.5 2.3 %attend.1.near = bf16[256,512]{1,0:T(8,128)(2,1)S(1)} custom-call(f32[1,128]{1,0:T(1,128)S(1)} %bitcast.10, f32[256,512]{1,0:T(8,128)S(1)} %q_late.2.first, bf16[256,512]{1,0:T(8,128)(2,1)S(1)} %collective-permute-done.22.landed, bf16[128,256]{1,0:T(8,128)(2,1)S(1)} %kv_join.1.refs_0_, bf16[128,256]{1,0:T(8,128)(2,1)S(1)} %collective-permute-done.23.refs_1_, ...), custom_call_target="tpu_custom_call" | custom-call | flops 268435456 | bytes 2097152 | tf_op jit(solution)/shard_map/attend/pallas_call | solution.py:122
  64.8 5.4 %collective-permute-done.28.near = bf16[256,512]{1,0:T(8,128)(2,1)S(1)} collective-permute-done((bf16[256,512]{1,0:T(8,128)(2,1)S(1)}, bf16[256,512]{1,0:T(8,128)(2,1)S(1)}, u32[]{:S(2)}, u32[]{:S(2)}) %collective-permute-start.28) | collective-permute-done | bytes 262176 | tf_op jit(solution)/shard_map/ppermute | solution.py:379
  71.8 1.2 %o_share.3 = (bf16[128,1024]{1,0:T(8,128)(2,1)S(1)}, bf16[128,1024]{1,0:T(8,128)(2,1)S(1)}) custom-call(s32[3]{0:T(128)S(1)} %copy-done.4, bf16[256,512]{1,0:T(8,128)(2,1)S(1)} %collective-permute-done.28.near, bf16[256,512]{1,0:T(8,128)(2,1)S(1)} %collective-permute-done.29.far, bf16[1024,512]{1,0:T(8,128)(2,1)S(1)} %copy-done, ...), custom_call_target="tpu_custom_call" | custom-call | flops 536870912 | bytes 2097152 | tf_op jit(solution)/shard_map/o_share/pallas_call | solution.py:122
  74.0 1.1 %collective-permute-start.35 = (bf16[128,1024]{1,0:T(8,128)(2,1)S(1)}, bf16[128,1024]{1,0:T(8,128)(2,1)S(1)}, u32[]{:S(2)}, u32[]{:S(2)}) collective-permute-start(bf16[128,1024]{1,0:T(8,128)(2,1)S(1)} %get-tuple-element.96), channel_id=1, source_target_pairs={{0,8},{4,12},{8,0},{12,4},{16,24},{20,28},{24,16},{28,20},{1,9},{5... | collective-permute-start | bytes 786440 | tf_op jit(solution)/shard_map/ppermute | solution.py:379
  75.1 1.2 %o_share.2 = (bf16[128,1024]{1,0:T(8,128)(2,1)S(1)}, bf16[128,1024]{1,0:T(8,128)(2,1)S(1)}) custom-call(s32[3]{0:T(128)S(1)} %copy-done.4, bf16[256,512]{1,0:T(8,128)(2,1)S(1)} %attend.1.near, bf16[256,512]{1,0:T(8,128)(2,1)S(1)} %collective-permute-done.26.far, bf16[1024,512]{1,0:T(8,128)(2,1)S(1)} %copy-done, ...), custom_call_target="tpu_custom_call" | custom-call | flops 536870912 | bytes 2097152 | tf_op jit(solution)/shard_map/o_share/pallas_call | solution.py:122
  76.4 5.9 %collective-permute-done.30.landed = bf16[128,1024]{1,0:T(8,128)(2,1)S(1)} collective-permute-done((bf16[128,1024]{1,0:T(8,128)(2,1)S(1)}, bf16[128,1024]{1,0:T(8,128)(2,1)S(1)}, u32[]{:S(2)}, u32[]{:S(2)}) %collective-permute-start.30) | collective-permute-done | bytes 262176 | tf_op jit(solution)/shard_map/ppermute | solution.py:379
  82.9 1.1 %collective-permute-start.31 = (bf16[128,512]{1,0:T(8,128)(2,1)S(1)}, bf16[128,512]{1,0:T(8,128)(2,1)S(1)}, u32[]{:S(2)}, u32[]{:S(2)}) collective-permute-start(bf16[128,512]{1,0:T(8,128)(2,1)S(1)} %get-tuple-element.92), channel_id=1, source_target_pairs={{0,1},{1,0},{2,3},{3,2},{4,5},{5,4},{6,7},{7,6},{8,9},{9,8},{10,11... | collective-permute-start | bytes 393224 | tf_op jit(solution)/shard_map/ppermute | solution.py:388
  84.0 2.6 %collective-permute-start.32 = (bf16[128,512]{1,0:T(8,128)(2,1)S(1)}, bf16[128,512]{1,0:T(8,128)(2,1)S(1)}, u32[]{:S(2)}, u32[]{:S(2)}) collective-permute-start(bf16[128,512]{1,0:T(8,128)(2,1)S(1)} %get-tuple-element.93), channel_id=1, source_target_pairs={{0,2},{1,3},{2,0},{3,1},{4,6},{5,7},{6,4},{7,5},{8,10},{9,11},{10,... | collective-permute-start | bytes 393224 | tf_op jit(solution)/shard_map/ppermute | solution.py:388
  89.0 3.4 %collective-permute-start.37 = (bf16[128,512]{1,0:T(8,128)(2,1)S(1)}, bf16[128,512]{1,0:T(8,128)(2,1)S(1)}, u32[]{:S(2)}, u32[]{:S(2)}) collective-permute-start(bf16[128,512]{1,0:T(8,128)(2,1)S(1)} %get-tuple-element.99), channel_id=1, source_target_pairs={{0,2},{1,3},{2,0},{3,1},{4,6},{5,7},{6,4},{7,5},{8,10},{9,11},{10,... | collective-permute-start | bytes 393224 | tf_op jit(solution)/shard_map/ppermute | solution.py:388
  93.2 4.1 %collective-permute-done.32.refs_2_ = bf16[128,512]{1,0:T(8,128)(2,1)S(1)} collective-permute-done((bf16[128,512]{1,0:T(8,128)(2,1)S(1)}, bf16[128,512]{1,0:T(8,128)(2,1)S(1)}, u32[]{:S(2)}, u32[]{:S(2)}) %collective-permute-start.32) | collective-permute-done | bytes 131104 | tf_op jit(solution)/shard_map/ppermute | solution.py:388
  97.4 9.7 %collective-permute-done.37.refs_2_ = bf16[128,512]{1,0:T(8,128)(2,1)S(1)} collective-permute-done((bf16[128,512]{1,0:T(8,128)(2,1)S(1)}, bf16[128,512]{1,0:T(8,128)(2,1)S(1)}, u32[]{:S(2)}, u32[]{:S(2)}) %collective-permute-start.37) | collective-permute-done | bytes 131104 | tf_op jit(solution)/shard_map/ppermute | solution.py:388
  107.2 1.3 %mix_keep.1 = bf16[128,1024]{1,0:T(8,128)(2,1)} custom-call(s32[3]{0:T(128)S(1)} %copy-done.4, f32[1]{0:T(128)S(6)} %tanh.3.gate, bf16[128,512]{1,0:T(8,128)(2,1)S(1)} %get-tuple-element.59.text, bf16[128,512]{1,0:T(8,128)(2,1)S(1)} %collective-permute-done.34.back, bf16[128,512]{1,0:T(8,128)(2,1)S(1)} %get-tuple-element.97.refs_0_, ...), custom_call_target="tpu_custom_call" | custom-call | flops 1048576 | bytes 1048576 | tf_op jit(solution)/shard_map/mix_keep/pallas_call | solution.py:122
  (96 shorter events, 22.7 us)
Async XLA Ops:
  0.0 17.6 %collective-permute-start.7 = (bf16[512,2048]{1,0:T(8,128)(2,1)}, bf16[512,2048]{1,0:T(8,128)(2,1)}, u32[]{:S(2)}, u32[]{:S(2)}) collective-permute-start(bf16[512,2048]{1,0:T(8,128)(2,1)} %refs_8_.1), channel_id=1, source_target_pairs={{0,4},{4,0},{8,12},{12,8},{16,20},{20,16},{24,28},{28,24},{1,5},{5... | collective-permute-start | bytes 6291464 | tf_op jit(solution)/shard_map/ppermute | solution.py:376
  5.2 4.8 %collective-permute-start = (bf16[16,1024]{1,0:T(8,128)(2,1)}, bf16[16,1024]{1,0:T(8,128)(2,1)S(1)}, u32[]{:S(2)}, u32[]{:S(2)}) collective-permute-start(bf16[16,1024]{1,0:T(8,128)(2,1)} %get-tuple-element.54), channel_id=1, source_target_pairs={{0,8},{4,12},{8,0},{12,4},{16,24},{20,28},{24,16},{28,20},{1,9},{5... | collective-permute-start | bytes 98312 | tf_op jit(solution)/shard_map/ppermute | solution.py:379
  7.7 4.1 %collective-permute-start.1 = (bf16[16,1024]{1,0:T(8,128)(2,1)}, bf16[16,1024]{1,0:T(8,128)(2,1)S(1)}, u32[]{:S(2)}, u32[]{:S(2)}) collective-permute-start(bf16[16,1024]{1,0:T(8,128)(2,1)} %get-tuple-element.55), channel_id=1, source_target_pairs={{0,16},{4,20},{8,24},{12,28},{16,0},{20,4},{24,8},{28,12},{1,17},{... | collective-permute-start | bytes 98312 | tf_op jit(solution)/shard_map/ppermute | solution.py:379
  9.2 5.0 %collective-permute-start.2 = (bf16[16,1024]{1,0:T(8,128)(2,1)}, bf16[16,1024]{1,0:T(8,128)(2,1)S(1)}, u32[]{:S(2)}, u32[]{:S(2)}) collective-permute-start(bf16[16,1024]{1,0:T(8,128)(2,1)} %get-tuple-element.56), channel_id=1, source_target_pairs={{0,24},{4,28},{8,16},{12,20},{16,8},{20,12},{24,0},{28,4},{1,25},{... | collective-permute-start | bytes 98312 | tf_op jit(solution)/shard_map/ppermute | solution.py:379
  14.3 14.3 %collective-permute-start.12 = (bf16[512,512]{1,0:T(8,128)(2,1)}, bf16[512,512]{1,0:T(8,128)(2,1)S(1)}, u32[]{:S(2)}, u32[]{:S(2)}) collective-permute-start(bf16[512,512]{1,0:T(8,128)(2,1)} %get-tuple-element.66.q_keep), channel_id=1, source_target_pairs={{0,8},{4,12},{8,0},{12,4},{16,24},{20,28},{24,16},{28,20},{1,9},{5... | collective-permute-start | bytes 1572872 | tf_op jit(solution)/shard_map/ppermute | solution.py:379
  14.8 16.8 %collective-permute-start.13 = (bf16[128,2048]{1,0:T(8,128)(2,1)}, bf16[128,2048]{1,0:T(8,128)(2,1)S(1)}, u32[]{:S(2)}, u32[]{:S(2)}) collective-permute-start(bf16[128,2048]{1,0:T(8,128)(2,1)} %get-tuple-element.67), channel_id=1, source_target_pairs={{0,16},{4,20},{8,24},{12,28},{16,0},{20,4},{24,8},{28,12},{1,17},{... | collective-permute-start | bytes 1572872 | tf_op jit(solution)/shard_map/ppermute | solution.py:379
  17.5 16.1 %collective-permute-start.15 = (bf16[512,512]{1,0:T(8,128)(2,1)}, bf16[512,512]{1,0:T(8,128)(2,1)S(1)}, u32[]{:S(2)}, u32[]{:S(2)}) collective-permute-start(bf16[512,512]{1,0:T(8,128)(2,1)} %get-tuple-element.71), channel_id=1, source_target_pairs={{0,4},{4,0},{8,12},{12,8},{16,20},{20,16},{24,28},{28,24},{1,5},{5... | collective-permute-start | bytes 1572872 | tf_op jit(solution)/shard_map/ppermute | solution.py:376
  21.2 11.8 %collective-permute-start.10 = (f32[32,1024]{1,0:T(8,128)S(1)}, f32[32,1024]{1,0:T(8,128)S(1)}, u32[]{:S(2)}, u32[]{:S(2)}) collective-permute-start(f32[32,1024]{1,0:T(8,128)S(1)} %get-tuple-element.62), channel_id=1, source_target_pairs={{0,16},{4,20},{8,24},{12,28},{16,0},{20,4},{24,8},{28,12},{1,17},{... | collective-permute-start | bytes 393224 | tf_op jit(solution)/shard_map/ppermute | solution.py:379
  23.2 9.8 %collective-permute-start.11 = (f32[32,1024]{1,0:T(8,128)S(1)}, f32[32,1024]{1,0:T(8,128)S(1)}, u32[]{:S(2)}, u32[]{:S(2)}) collective-permute-start(f32[32,1024]{1,0:T(8,128)S(1)} %get-tuple-element.63), channel_id=1, source_target_pairs={{0,24},{4,28},{8,16},{12,20},{16,8},{20,12},{24,0},{28,4},{1,25},{... | collective-permute-start | bytes 393224 | tf_op jit(solution)/shard_map/ppermute | solution.py:379
  28.5 5.0 %collective-permute-start.9 = (f32[32,1024]{1,0:T(8,128)S(1)}, f32[32,1024]{1,0:T(8,128)S(1)}, u32[]{:S(2)}, u32[]{:S(2)}) collective-permute-start(f32[32,1024]{1,0:T(8,128)S(1)} %get-tuple-element.61), channel_id=1, source_target_pairs={{0,8},{4,12},{8,0},{12,4},{16,24},{20,28},{24,16},{28,20},{1,9},{5... | collective-permute-start | bytes 393224 | tf_op jit(solution)/shard_map/ppermute | solution.py:379
  33.5 4.1 %collective-permute-start.18 = (bf16[128,2048]{1,0:T(8,128)(2,1)S(1)}, bf16[128,2048]{1,0:T(8,128)(2,1)S(1)}, u32[]{:S(2)}, u32[]{:S(2)}) collective-permute-start(bf16[128,2048]{1,0:T(8,128)(2,1)S(1)} %collective-permute-done.13.own), channel_id=1, source_target_pairs={{0,4},{4,0},{8,12},{12,8},{16,20},{20,16},{24,28},{28,24},{1,5},{5... | collective-permute-start | bytes 1572872 | tf_op jit(solution)/shard_map/ppermute | solution.py:376
  33.6 14.4 %collective-permute-start.16 = (bf16[512,512]{1,0:T(8,128)(2,1)S(1)}, bf16[512,512]{1,0:T(8,128)(2,1)S(1)}, u32[]{:S(2)}, u32[]{:S(2)}) collective-permute-start(bf16[512,512]{1,0:T(8,128)(2,1)S(1)} %collective-permute-done.15.q_other), channel_id=1, source_target_pairs={{0,8},{4,12},{8,0},{12,4},{16,24},{20,28},{24,16},{28,20},{1,9},{5... | collective-permute-start | bytes 1572872 | tf_op jit(solution)/shard_map/ppermute | solution.py:379
  37.0 16.8 %collective-permute-start.17 = (bf16[512,512]{1,0:T(8,128)(2,1)S(1)}, bf16[512,512]{1,0:T(8,128)(2,1)S(1)}, u32[]{:S(2)}, u32[]{:S(2)}) collective-permute-start(bf16[512,512]{1,0:T(8,128)(2,1)S(1)} %get-tuple-element.78), channel_id=1, source_target_pairs={{0,16},{4,20},{8,24},{12,28},{16,0},{20,4},{24,8},{28,12},{1,17},{... | collective-permute-start | bytes 1572872 | tf_op jit(solution)/shard_map/ppermute | solution.py:379
  37.6 15.2 %collective-permute-start.14 = (bf16[128,2048]{1,0:T(8,128)(2,1)S(1)}, bf16[128,2048]{1,0:T(8,128)(2,1)S(1)}, u32[]{:S(2)}, u32[]{:S(2)}) collective-permute-start(bf16[128,2048]{1,0:T(8,128)(2,1)S(1)} %get-tuple-element.69.own), channel_id=1, source_target_pairs={{0,4},{4,0},{8,12},{12,8},{16,20},{20,16},{24,28},{28,24},{1,5},{5... | collective-permute-start | bytes 1572872 | tf_op jit(solution)/shard_map/ppermute | solution.py:376
  39.3 4.8 %collective-permute-start.20 = (bf16[64,256]{1,0:T(8,128)(2,1)S(1)}, bf16[64,256]{1,0:T(8,128)(2,1)S(1)}, u32[]{:S(2)}, u32[]{:S(2)}) collective-permute-start(bf16[64,256]{1,0:T(8,128)(2,1)S(1)} %kv_turn.1), channel_id=1, source_target_pairs={{0,2},{1,3},{2,0},{3,1},{4,6},{5,7},{6,4},{7,5},{8,10},{9,11},{10,... | collective-permute-start | bytes 98312 | tf_op jit(solution)/shard_map/ppermute | solution.py:388
  44.2 8.1 %collective-permute-start.21 = (bf16[128,256]{1,0:T(8,128)(2,1)S(1)}, bf16[128,256]{1,0:T(8,128)(2,1)S(1)}, u32[]{:S(2)}, u32[]{:S(2)}) collective-permute-start(bf16[128,256]{1,0:T(8,128)(2,1)S(1)} %kv_join.1.refs_0_), channel_id=1, source_target_pairs={{0,16},{4,20},{8,24},{12,28},{16,0},{20,4},{24,8},{28,12},{1,17},{... | collective-permute-start | bytes 196616 | tf_op jit(solution)/shard_map/ppermute | solution.py:379
  49.0 7.4 %collective-permute-start.23 = (bf16[128,256]{1,0:T(8,128)(2,1)S(1)}, bf16[128,256]{1,0:T(8,128)(2,1)S(1)}, u32[]{:S(2)}, u32[]{:S(2)}) collective-permute-start(bf16[128,256]{1,0:T(8,128)(2,1)S(1)} %kv_join.1.refs_0_), channel_id=1, source_target_pairs={{0,8},{4,12},{8,0},{12,4},{16,24},{20,28},{24,16},{28,20},{1,9},{5... | collective-permute-start | bytes 196616 | tf_op jit(solution)/shard_map/ppermute | solution.py:379
  50.0 6.4 %collective-permute-start.24 = (bf16[128,256]{1,0:T(8,128)(2,1)S(1)}, bf16[128,256]{1,0:T(8,128)(2,1)S(1)}, u32[]{:S(2)}, u32[]{:S(2)}) collective-permute-start(bf16[128,256]{1,0:T(8,128)(2,1)S(1)} %kv_join.1.refs_0_), channel_id=1, source_target_pairs={{0,24},{4,28},{8,16},{12,20},{16,8},{20,12},{24,0},{28,4},{1,25},{... | collective-permute-start | bytes 196616 | tf_op jit(solution)/shard_map/ppermute | solution.py:379
  52.2 9.2 %collective-permute-start.22 = (bf16[256,512]{1,0:T(8,128)(2,1)S(1)}, bf16[256,512]{1,0:T(8,128)(2,1)S(1)}, u32[]{:S(2)}, u32[]{:S(2)}) collective-permute-start(bf16[256,512]{1,0:T(8,128)(2,1)S(1)} %q_late.3), channel_id=1, source_target_pairs={{0,16},{4,20},{8,24},{12,28},{16,0},{20,4},{24,8},{28,12},{1,17},{... | collective-permute-start | bytes 786440 | tf_op jit(solution)/shard_map/ppermute | solution.py:379
  54.8 16.6 %collective-permute-start.27 = (bf16[512,512]{1,0:T(8,128)(2,1)S(1)}, bf16[512,512]{1,0:T(8,128)(2,1)S(1)}, u32[]{:S(2)}, u32[]{:S(2)}) collective-permute-start(bf16[512,512]{1,0:T(8,128)(2,1)S(1)} %get-tuple-element.88), channel_id=1, source_target_pairs={{0,16},{4,20},{8,24},{12,28},{16,0},{20,4},{24,8},{28,12},{1,17},{... | collective-permute-start | bytes 1572872 | tf_op jit(solution)/shard_map/ppermute | solution.py:379
  63.8 6.4 %collective-permute-start.28 = (bf16[256,512]{1,0:T(8,128)(2,1)S(1)}, bf16[256,512]{1,0:T(8,128)(2,1)S(1)}, u32[]{:S(2)}, u32[]{:S(2)}) collective-permute-start(bf16[256,512]{1,0:T(8,128)(2,1)S(1)} %attend.1.near), channel_id=1, source_target_pairs={{0,8},{4,12},{8,0},{12,4},{16,24},{20,28},{24,16},{28,20},{1,9},{5... | collective-permute-start | bytes 786440 | tf_op jit(solution)/shard_map/ppermute | solution.py:379
  70.3 4.9 %collective-permute-start.26 = (bf16[256,512]{1,0:T(8,128)(2,1)S(1)}, bf16[256,512]{1,0:T(8,128)(2,1)S(1)}, u32[]{:S(2)}, u32[]{:S(2)}) collective-permute-start(bf16[256,512]{1,0:T(8,128)(2,1)S(1)} %attend.1.near), channel_id=1, source_target_pairs={{0,4},{4,0},{8,12},{12,8},{16,20},{20,16},{24,28},{28,24},{1,5},{5... | collective-permute-start | bytes 786440 | tf_op jit(solution)/shard_map/ppermute | solution.py:376
  73.0 9.2 %collective-permute-start.30 = (bf16[128,1024]{1,0:T(8,128)(2,1)S(1)}, bf16[128,1024]{1,0:T(8,128)(2,1)S(1)}, u32[]{:S(2)}, u32[]{:S(2)}) collective-permute-start(bf16[128,1024]{1,0:T(8,128)(2,1)S(1)} %get-tuple-element.90), channel_id=1, source_target_pairs={{0,8},{4,12},{8,0},{12,4},{16,24},{20,28},{24,16},{28,20},{1,9},{5... | collective-permute-start | bytes 786440 | tf_op jit(solution)/shard_map/ppermute | solution.py:379
  74.0 14.0 %collective-permute-start.35 = (bf16[128,1024]{1,0:T(8,128)(2,1)S(1)}, bf16[128,1024]{1,0:T(8,128)(2,1)S(1)}, u32[]{:S(2)}, u32[]{:S(2)}) collective-permute-start(bf16[128,1024]{1,0:T(8,128)(2,1)S(1)} %get-tuple-element.96), channel_id=1, source_target_pairs={{0,8},{4,12},{8,0},{12,4},{16,24},{20,28},{24,16},{28,20},{1,9},{5... | collective-permute-start | bytes 786440 | tf_op jit(solution)/shard_map/ppermute | solution.py:379
  75.1 13.9 %collective-permute-start.8 = (bf16[128,512]{1,0:T(8,128)(2,1)S(1)}, bf16[128,512]{1,0:T(8,128)(2,1)S(1)}, u32[]{:S(2)}, u32[]{:S(2)}) collective-permute-start(bf16[128,512]{1,0:T(8,128)(2,1)S(1)} %get-tuple-element.60), channel_id=1, source_target_pairs={{0,4},{4,0},{8,12},{12,8},{16,20},{20,16},{24,28},{28,24},{1,5},{5... | collective-permute-start | bytes 393224 | tf_op jit(solution)/shard_map/ppermute | solution.py:376
  82.9 9.5 %collective-permute-start.31 = (bf16[128,512]{1,0:T(8,128)(2,1)S(1)}, bf16[128,512]{1,0:T(8,128)(2,1)S(1)}, u32[]{:S(2)}, u32[]{:S(2)}) collective-permute-start(bf16[128,512]{1,0:T(8,128)(2,1)S(1)} %get-tuple-element.92), channel_id=1, source_target_pairs={{0,1},{1,0},{2,3},{3,2},{4,5},{5,4},{6,7},{7,6},{8,9},{9,8},{10,11... | collective-permute-start | bytes 393224 | tf_op jit(solution)/shard_map/ppermute | solution.py:388
  84.0 13.2 %collective-permute-start.32 = (bf16[128,512]{1,0:T(8,128)(2,1)S(1)}, bf16[128,512]{1,0:T(8,128)(2,1)S(1)}, u32[]{:S(2)}, u32[]{:S(2)}) collective-permute-start(bf16[128,512]{1,0:T(8,128)(2,1)S(1)} %get-tuple-element.93), channel_id=1, source_target_pairs={{0,2},{1,3},{2,0},{3,1},{4,6},{5,7},{6,4},{7,5},{8,10},{9,11},{10,... | collective-permute-start | bytes 393224 | tf_op jit(solution)/shard_map/ppermute | solution.py:388
  86.6 10.6 %collective-permute-start.33 = (bf16[128,512]{1,0:T(8,128)(2,1)S(1)}, bf16[128,512]{1,0:T(8,128)(2,1)S(1)}, u32[]{:S(2)}, u32[]{:S(2)}) collective-permute-start(bf16[128,512]{1,0:T(8,128)(2,1)S(1)} %get-tuple-element.94), channel_id=1, source_target_pairs={{0,3},{1,2},{2,1},{3,0},{4,7},{5,6},{6,5},{7,4},{8,11},{9,10},{10,... | collective-permute-start | bytes 393224 | tf_op jit(solution)/shard_map/ppermute | solution.py:388
  88.7 8.7 %collective-permute-start.36 = (bf16[128,512]{1,0:T(8,128)(2,1)S(1)}, bf16[128,512]{1,0:T(8,128)(2,1)S(1)}, u32[]{:S(2)}, u32[]{:S(2)}) collective-permute-start(bf16[128,512]{1,0:T(8,128)(2,1)S(1)} %get-tuple-element.98), channel_id=1, source_target_pairs={{0,1},{1,0},{2,3},{3,2},{4,5},{5,4},{6,7},{7,6},{8,9},{9,8},{10,11... | collective-permute-start | bytes 393224 | tf_op jit(solution)/shard_map/ppermute | solution.py:388
  89.0 18.1 %collective-permute-start.37 = (bf16[128,512]{1,0:T(8,128)(2,1)S(1)}, bf16[128,512]{1,0:T(8,128)(2,1)S(1)}, u32[]{:S(2)}, u32[]{:S(2)}) collective-permute-start(bf16[128,512]{1,0:T(8,128)(2,1)S(1)} %get-tuple-element.99), channel_id=1, source_target_pairs={{0,2},{1,3},{2,0},{3,1},{4,6},{5,7},{6,4},{7,5},{8,10},{9,11},{10,... | collective-permute-start | bytes 393224 | tf_op jit(solution)/shard_map/ppermute | solution.py:388
  92.4 14.7 %collective-permute-start.38 = (bf16[128,512]{1,0:T(8,128)(2,1)S(1)}, bf16[128,512]{1,0:T(8,128)(2,1)S(1)}, u32[]{:S(2)}, u32[]{:S(2)}) collective-permute-start(bf16[128,512]{1,0:T(8,128)(2,1)S(1)} %get-tuple-element.100), channel_id=1, source_target_pairs={{0,3},{1,2},{2,1},{3,0},{4,7},{5,6},{6,5},{7,4},{8,11},{9,10},{10,... | collective-permute-start | bytes 393224 | tf_op jit(solution)/shard_map/ppermute | solution.py:388
  97.3 9.8 %collective-permute-start.34 = (bf16[128,512]{1,0:T(8,128)(2,1)S(1)}, bf16[128,512]{1,0:T(8,128)(2,1)S(1)}, u32[]{:S(2)}, u32[]{:S(2)}) collective-permute-start(bf16[128,512]{1,0:T(8,128)(2,1)S(1)} %mix_give.1), channel_id=1, source_target_pairs={{0,4},{4,0},{8,12},{12,8},{16,20},{20,16},{24,28},{28,24},{1,5},{5... | collective-permute-start | bytes 393224 | tf_op jit(solution)/shard_map/ppermute | solution.py:376
  (19 other events, 148.2 us)

commit v2 on v0

--- a/solution.py
+++ b/solution.py
@@ -136,10 +136,8 @@
     return pl.ds(pl.multiple_of(index * size, size), size)
 
 
-def row_scales(text, scale, step, ready=()):
-    for k, r in enumerate(range(0, text.shape[0], step)):
-        if ready:
-            ready[k].wait()
+def row_scales(text, scale, step):
+    for r in range(0, text.shape[0], step):
         x = text[r : r + step, :].astype(F32)
         mean_sq = jnp.mean(x * x, axis=-1, keepdims=True)
         scale[r : r + step, :] = jnp.broadcast_to(lax.rsqrt(mean_sq + EPS), (step, 128))
@@ -153,39 +151,11 @@
         out[r : r + step, :] = (x * scale[r : r + step, 0:1] * row_gain).astype(BF16)
 
 
-def start_kernel(where, text_hbm, gain, vis_hbm, q_hbm, *refs):
-    pieces, refs = refs[:CHIPS], refs[CHIPS:]
-    far, q_keep, q_give, text, vis, scale, sems = refs
-    chip, core = where[0], where[1]
-    tokens = text.shape[0]
-    half = q_keep.shape[1]
-    step = 16
-    first = pltpu.make_async_copy(vis_hbm, vis, sems.at[0])
-    first.start()
-    copies = []
-    for k, r in enumerate(range(0, tokens, step)):
-        rows = pl.ds(r, step)
-        copies.append(pltpu.make_async_copy(text_hbm.at[rows, :], text.at[rows, :], sems.at[3 + k]))
-        copies[-1].start()
-    cuts = [
-        pltpu.make_async_copy(q_hbm.at[:, block(core, half)], q_keep, sems.at[1]),
-        pltpu.make_async_copy(q_hbm.at[:, block(1 - core, half)], q_give, sems.at[2]),
-    ]
-    for copy in cuts:
-        copy.start()
-    first.wait()
-    for s in range(CHIPS):
-        pieces[s][...] = vis[:, block(chip ^ s, pieces[s].shape[1])]
-    row_scales(text, scale, step, copies)
-    scaled(text, scale, gain, far, 1 - chip // 2, step)
-    for copy in cuts:
-        copy.wait()
-
-
-def near_kernel(where, text, gain, near, text_keep, text_give, scale):
+def spread_kernel(where, text, gain, near, far, text_keep, text_give, scale):
     chip, core, plane = where[0], where[1], where[2]
     half = text_keep.shape[1]
     row_scales(text, scale, 16)
+    scaled(text, scale, gain, far, 1 - chip // 2, 16)
     scaled(text, scale, gain, near, chip // 2, 16)
     text_keep[...] = text[:, block(2 * plane + core, half)]
     text_give[...] = text[:, block(2 * plane + 1 - core, half)]
@@ -208,7 +178,8 @@
             )
         )
         copies[-1].start()
-    near, far = block(core, rows), block(1 - core, rows)
+    first = 2 * where[0]
+    near, far = block(first + core, rows), block(first + 1 - core, rows)
     x_near = jnp.concatenate([x[:, near] for x in vis + vis_other], axis=0)
     x_far = jnp.concatenate([x[:, far] for x in vis + vis_other], axis=0)
     count = vis[0].shape[0]
@@ -252,25 +223,26 @@
     out[2 * lines :, :] = last[...]
 
 
-def query_share(index, own, other, first, second, flip):
-    rows = first.shape[0]
+def query_share(index, own, other, first, second, core):
+    rows, width = first.shape
+    half = block(core, width // 2)
     total = None
-    for weight, k in ((first, index), (second, index ^ flip)):
+    for weight, k in ((first, index), (second, index ^ 1)):
         cols = block(k, rows)
         x = jnp.concatenate((own[:, cols], other[:, cols]), axis=0)
-        share = jnp.dot(x, weight[...], preferred_element_type=F32)
+        share = jnp.dot(x, weight[:, half], preferred_element_type=F32)
         total = share if total is None else total + share
     return total
 
 
-def early_kernel(where, own, other, q_keep, q_other, out):
+def early_kernel(where, own, other, q_own, q_other, out):
     index = 2 * lax.rem(where[0], 2) + where[1]
-    out[...] = query_share(index, own, other, q_keep, q_other, 1)
+    out[...] = query_share(index, own, other, q_own, q_other, where[1])
 
 
 def late_kernel(where, own, other, q_side, q_corner, early, out):
     index = (2 * lax.rem(where[0], 2) + where[1]) ^ 2
-    share = early[...] + query_share(index, own, other, q_side, q_corner, 1)
+    share = early[...] + query_share(index, own, other, q_side, q_corner, where[1])
     out[...] = share.astype(out.dtype)
 
 
@@ -321,7 +293,7 @@
 
             @pl.when((first ^ t) == s)
             def _():
-                outs[t][...] = (own, landed)[s % 2][:, (s // 2) * half : (s // 2 + 1) * half]
+                outs[t][...] = (own, landed)[s // 2][:, (s % 2) * half : (s % 2 + 1) * half]
 
 
 def mixed_rows(gate, text, shares):
@@ -391,29 +363,25 @@
     vis = vision.reshape(vis_here, width)
     kv_other = swap(kv_weight)
 
-    anywhere = pl.BlockSpec(memory_space=pl.ANY)
-    *vis_pieces, far, q_keep, q_give = call(
-        start_kernel,
-        (where, text, input_gain[None], vis, q_weight),
-        [SMEM, anywhere, VMEM, anywhere, anywhere],
-        [shape(vis_here, part)] * CHIPS
-        + [shape(tokens, width // 2)]
-        + [shape(rows_dev, half)] * 2,
-        out_specs=[VMEM] * (1 + CHIPS) + [anywhere] * 2,
-        scratch=[
-            pltpu.VMEM((tokens, width), BF16),
-            pltpu.VMEM((vis_here, width), BF16),
-            pltpu.VMEM((tokens, 128), F32),
-            pltpu.SemaphoreType.DMA((3 + tokens // 16,)),
-        ],
+    vis_own = [vis] + [peer(vis, s) for s in (1, 3, 2)]
+    vis_own = [vis_own[0], vis_own[1], vis_own[3], vis_own[2]]
+    vis_other = [swap(x) for x in vis_own]
+    q_other = swap(q_weight)
+    q_sent, _ = lax.optimization_barrier((q_weight, (vis_own[1], vis_own[3])))
+    q_side = along_x(q_sent)
+
+    where_text, _ = lax.optimization_barrier((where, vis_own[1]))
+    near, far, text_keep, text_give = call(
+        spread_kernel,
+        (where_text, text, input_gain[None]),
+        [SMEM] + [VMEM] * 2,
+        [shape(tokens, width // 2)] * 2 + [shape(tokens, half)] * 2,
+        scratch=[pltpu.VMEM((tokens, 128), F32)],
         flops=8 * tokens * width,
         size=4 * 2**20,
-        name="start",
-        limit=60,
-    )
-    vis_own = [vis_pieces[0]] + [peer(vis_pieces[s], s) for s in steps]
-    vis_other = [swap(x) for x in vis_own]
-    q_side, q_other = along_x(q_keep), swap(q_give)
+        name="spread",
+    )
+    far, _ = lax.optimization_barrier((far, vis_own[2]))
     far = along_y(far)
 
     shares = call(
@@ -430,19 +398,9 @@
         size=4 * 2**20,
         name="kv_shares",
     )
-    where_near, _ = lax.optimization_barrier((where, shares[0]))
-    near, text_keep, text_give = call(
-        near_kernel,
-        (where_near, text, input_gain[None]),
-        [SMEM, VMEM, VMEM],
-        [shape(tokens, width // 2)] + [shape(tokens, half)] * 2,
-        scratch=[pltpu.VMEM((tokens, 128), F32)],
-        flops=8 * tokens * width,
-        size=4 * 2**20,
-        name="near",
-    )
     shares = [shares[0]] + [peer(shares[s], s) for s in steps]
-    shares[3], q_side, far, near = lax.optimization_barrier((shares[3], q_side, far, near))
+    shares, far, q_side = lax.optimization_barrier((shares, far, q_side))
+    q_corner = swap(q_side)
     here, there, give = call(
         kv_norm_kernel,
         (where, k_gain[None], *shares),
@@ -454,7 +412,7 @@
     early = [
         call(
             early_kernel,
-            (where, *pair, q_keep, q_other),
+            (where, *pair, q_weight, q_other),
             [SMEM] + [VMEM] * 4,
             [shape(2 * tokens, half, F32)],
             flops=4 * tokens * part * half,
@@ -463,8 +421,22 @@
         )[0]
         for pair in blocks
     ]
-    kv_z = across(give, 1)
-    kv_z, early[0] = lax.optimization_barrier((kv_z, early[0]))
+    o_early, _ = lax.optimization_barrier((o_weight[:half], here))
+    o_early = along_x(o_early)
+    early[1], o_early = lax.optimization_barrier((early[1], o_early))
+    q_far, q_first = [
+        call(
+            late_kernel,
+            (where, *blocks[k], q_side, q_corner, early[k]),
+            [SMEM] + [VMEM] * 5,
+            [shape(2 * tokens, half, kind)],
+            flops=4 * tokens * part * half,
+            size=2 * 2**20,
+            name="q_late",
+        )[0]
+        for k, kind in ((0, BF16), (1, F32))
+    ]
+    kv_z, q_far = lax.optimization_barrier((across(give, 1), q_far))
     turn = call(
         kv_turn_kernel,
         (there, kv_z),
@@ -481,27 +453,10 @@
     )[0]
     kv_all = [kv_first] + [peer(kv_first, s) for s in steps]
 
-    q_behind, _ = lax.optimization_barrier((q_other, shares[0]))
-    q_corner = along_x(q_behind)
-
-    o_early, _ = lax.optimization_barrier((o_weight[:half], here))
-    q_corner, o_early = lax.optimization_barrier((q_corner, along_y(o_early)))
-    early[1], kv_all[1] = lax.optimization_barrier((early[1], kv_all[1]))
-    q_far, q_first = [
-        call(
-            late_kernel,
-            (where, *blocks[k], q_side, q_corner, early[k]),
-            [SMEM] + [VMEM] * 5,
-            [shape(2 * tokens, half, kind)],
-            flops=4 * tokens * part * half,
-            size=2 * 2**20,
-            name="q_late",
-        )[0]
-        for k, kind in ((0, BF16), (1, F32))
-    ]
+
     landed = along_y(q_far)
-    o_late, _ = lax.optimization_barrier((o_weight[half:], q_far))
-    o_late = along_y(o_late)
+    o_late, _ = lax.optimization_barrier((o_weight[half:], kv_all[1]))
+    o_late = along_x(o_late)
 
     ids = jnp.concatenate((segment_ids, swap(segment_ids)))
     images = jnp.arange(image_slot.shape[0])
@@ -528,7 +483,7 @@
         name="attend",
     )[0]
 
-    context_x = along_x(context)
+    context_y = along_y(context)
     shares = [
         call(
             out_kernel,
@@ -539,13 +494,13 @@
             size=2 * 2**20,
             name="o_share",
         )
-        for x in (context_x, context)
+        for x in (context_y, context)
     ]
     summands = []
     for rows in (1, 0):
         picked = call(
             pick_kernel,
-            (where, shares[1][rows], along_x(shares[0][rows])),
+            (where, shares[1][rows], along_y(shares[0][rows])),
             [SMEM] + [VMEM] * 2,
             [shape(tokens, half)] * CHIPS,
             flops=2**20,

time: 147 us -> 111 us (0.76)
  Pallas kernels: 50.1 us -> 15.1 us
  local copies, waits for them, and re-layouts: 0.98 us -> 4.54 us
  waiting for transfers between devices: 54.5 us -> 51.6 us
    pallas_call x17 -> x16, Pallas kernels: 50.1 us -> 15.1 us  [call(): pl.pallas_call(kernel, out_shape=outs, in_specs=specs, out_specs=[VMEM] *...]
    ppermute x18 -> x17, waiting for transfers between devices: 36.7 us -> 32.5 us  [peer(): return lax.ppermute(x, 'ctx', [(k, k ^ 2 * s) for k in range(ctx_count)])]
    unnamed x24 -> x22, local copies, waits for them, and re-layouts: 0.91 us -> 4.47 us
    ppermute x13 -> x14, waiting for transfers between devices: 2.64 us -> 4.3 us  [swap(): return lax.ppermute(x, 'ctx', [(k, k ^ 1) for k in range(ctx_count)])]
    ppermute x18 -> x17, starting transfers between devices: 23.1 us -> 22.3 us  [peer(): return lax.ppermute(x, 'ctx', [(k, k ^ 2 * s) for k in range(ctx_count)])]
    ppermute x13 -> x14, starting transfers between devices: 2.73 us -> 3.14 us  [swap(): return lax.ppermute(x, 'ctx', [(k, k ^ 1) for k in range(ctx_count)])]
  transfers between devices with their start and end apart: 39 -> 39, of which waited for: 13 -> 20; matrix products, arithmetic and copies ran while one was open for 1% -> 1% of each run, Pallas kernels for 33% -> 12%
where the time goes in v2:
time: 111 us
  waiting for transfers between devices  51.6 us (46%)
  starting transfers between devices  38.5 us (35%)
  Pallas kernels  15.1 us (14%)
  local copies, waits for them, and re-layouts  4.54 us (4%)
    ppermute x17, waiting for transfers between devices, peer(): return lax.ppermute(x, 'ctx', [(k, k ^ 2 * s) for k in range(ctx_count)])  32.5 us
    ppermute x17, starting transfers between devices, peer(): return lax.ppermute(x, 'ctx', [(k, k ^ 2 * s) for k in range(ctx_count)])  22.3 us
    pallas_call x16, Pallas kernels, call(): pl.pallas_call(kernel, out_shape=outs, in_specs=specs, out_specs=[VMEM] *...  15.1 us
    ppermute x8, waiting for transfers between devices, across(): return lax.ppermute(x, 'img', [(k, k ^ t) for k in range(CHIPS)])  14.8 us
    ppermute x8, starting transfers between devices, across(): return lax.ppermute(x, 'img', [(k, k ^ t) for k in range(CHIPS)])  13.1 us
    unnamed x22, local copies, waits for them, and re-layouts  4.47 us
    ppermute x14, waiting for transfers between devices, swap(): return lax.ppermute(x, 'ctx', [(k, k ^ 1) for k in range(ctx_count)])  4.3 us
    ppermute x14, starting transfers between devices, swap(): return lax.ppermute(x, 'ctx', [(k, k ^ 1) for k in range(ctx_count)])  3.14 us
  transfers between devices with their start and end apart: 39, of which 20 were waited for; matrix products, arithmetic and copies ran while one was open for 1% of the time, Pallas kernels for 12%

profile of v2, /device:TPU:0, one launch (start us, length us, event | category | flops | bytes accessed | tf_op | source)
XLA Modules:
  0.0 111.2 jit_solution(1079343481866410387)
XLA Ops:
  0.5 2.5 %collective-permute-start = (bf16[16,4096]{1,0:T(8,128)(2,1)}, bf16[16,4096]{1,0:T(8,128)(2,1)S(1)}, u32[]{:S(2)}, u32[]{:S(2)}) collective-permute-start(bf16[16,4096]{1,0:T(8,128)(2,1)} %bitcast.7), channel_id=1, source_target_pairs={{0,8},{4,12},{8,0},{12,4},{16,24},{20,28},{24,16},{28,20},{1,9},{5... | collective-permute-start | bytes 393224 | tf_op jit(solution)/shard_map/ppermute | solution.py:351
  2.9 1.5 %collective-permute-start.4 = (bf16[16,4096]{1,0:T(8,128)(2,1)}, bf16[16,4096]{1,0:T(8,128)(2,1)S(1)}, u32[]{:S(2)}, u32[]{:S(2)}) collective-permute-start(bf16[16,4096]{1,0:T(8,128)(2,1)} %bitcast.8), channel_id=1, source_target_pairs={{0,24},{4,28},{8,16},{12,20},{16,8},{20,12},{24,0},{28,4},{1,25},{... | collective-permute-start | bytes 393224 | tf_op jit(solution)/shard_map/ppermute | solution.py:351
  4.4 3.1 %collective-permute-done.refs_1_ = bf16[16,4096]{1,0:T(8,128)(2,1)S(1)} collective-permute-done((bf16[16,4096]{1,0:T(8,128)(2,1)}, bf16[16,4096]{1,0:T(8,128)(2,1)S(1)}, u32[]{:S(2)}, u32[]{:S(2)}) %collective-permute-start) | collective-permute-done | bytes 131104 | tf_op jit(solution)/shard_map/ppermute | solution.py:351
  7.5 3.8 %collective-permute-done.4.refs_3_ = bf16[16,4096]{1,0:T(8,128)(2,1)S(1)} collective-permute-done((bf16[16,4096]{1,0:T(8,128)(2,1)}, bf16[16,4096]{1,0:T(8,128)(2,1)S(1)}, u32[]{:S(2)}, u32[]{:S(2)}) %collective-permute-start.4) | collective-permute-done | bytes 131104 | tf_op jit(solution)/shard_map/ppermute | solution.py:351
  11.3 1.5 %collective-permute-start.14 = (bf16[512,1024]{1,0:T(8,128)(2,1)}, bf16[512,1024]{1,0:T(8,128)(2,1)S(1)}, u32[]{:S(2)}, u32[]{:S(2)}) collective-permute-start(bf16[512,1024]{1,0:T(8,128)(2,1)} %q_own.3), channel_id=1, source_target_pairs={{0,8},{4,12},{8,0},{12,4},{16,24},{20,28},{24,16},{28,20},{1,9},{5... | collective-permute-start | bytes 3145736 | tf_op jit(solution)/shard_map/ppermute | solution.py:351
  16.4 1.6 %collective-permute-done.3.refs_2_ = bf16[16,4096]{1,0:T(8,128)(2,1)S(1)} collective-permute-done((bf16[16,4096]{1,0:T(8,128)(2,1)}, bf16[16,4096]{1,0:T(8,128)(2,1)S(1)}, u32[]{:S(2)}, u32[]{:S(2)}) %collective-permute-start.3) | collective-permute-done | bytes 131104 | tf_op jit(solution)/shard_map/ppermute | solution.py:351
  21.8 1.6 %copy-done.2 = bf16[512,2048]{1,0:T(8,128)(2,1)S(1)} copy-done((bf16[512,2048]{1,0:T(8,128)(2,1)S(1)}, bf16[512,2048]{1,0:T(8,128)(2,1)}, u32[]{:S(2)}) %copy-start.2) | copy-done | bytes 2097176
  24.3 1.8 %kv_shares.1 = (f32[32,1024]{1,0:T(8,128)S(1)}, f32[32,1024]{1,0:T(8,128)S(1)}, f32[32,1024]{1,0:T(8,128)S(1)}, f32[32,1024]{1,0:T(8,128)S(1)}) custom-call(s32[3]{0:T(128)S(1)} %pad_add_fusion.1.where, bf16[16,4096]{1,0:T(8,128)(2,1)S(1)} %bitcast.11, bf16[16,4096]{1,0:T(8,128)(2,1)S(1)} %collective-permute-done.refs_1_, ...), custom_call_target="tpu_custom_call" | custom-call | flops 536870912 | bytes 4194304 | tf_op jit(solution)/shard_map/kv_shares/pallas_call | solution.py:122
  26.5 1.8 %collective-permute-start.11 = (f32[32,1024]{1,0:T(8,128)S(1)}, f32[32,1024]{1,0:T(8,128)S(1)}, u32[]{:S(2)}, u32[]{:S(2)}) collective-permute-start(f32[32,1024]{1,0:T(8,128)S(1)} %get-tuple-element.49), channel_id=1, source_target_pairs={{0,16},{4,20},{8,24},{12,28},{16,0},{20,4},{24,8},{28,12},{1,17},{... | collective-permute-start | bytes 393224 | tf_op jit(solution)/shard_map/ppermute | solution.py:351
  28.3 1.4 %collective-permute-start.12 = (f32[32,1024]{1,0:T(8,128)S(1)}, f32[32,1024]{1,0:T(8,128)S(1)}, u32[]{:S(2)}, u32[]{:S(2)}) collective-permute-start(f32[32,1024]{1,0:T(8,128)S(1)} %get-tuple-element.50), channel_id=1, source_target_pairs={{0,24},{4,28},{8,16},{12,20},{16,8},{20,12},{24,0},{28,4},{1,25},{... | collective-permute-start | bytes 393224 | tf_op jit(solution)/shard_map/ppermute | solution.py:351
  29.7 1.9 %collective-permute-done.13.own = bf16[128,2048]{1,0:T(8,128)(2,1)S(1)} collective-permute-done((bf16[128,2048]{1,0:T(8,128)(2,1)S(1)}, bf16[128,2048]{1,0:T(8,128)(2,1)S(1)}, u32[]{:S(2)}, u32[]{:S(2)}) %collective-permute-start.13) | collective-permute-done | bytes 524320 | tf_op jit(solution)/shard_map/ppermute | solution.py:351
  31.7 5.9 %collective-permute-done.14.q_side = bf16[512,1024]{1,0:T(8,128)(2,1)S(1)} collective-permute-done((bf16[512,1024]{1,0:T(8,128)(2,1)}, bf16[512,1024]{1,0:T(8,128)(2,1)S(1)}, u32[]{:S(2)}, u32[]{:S(2)}) %collective-permute-start.14) | collective-permute-done | bytes 1048608 | tf_op jit(solution)/shard_map/ppermute | solution.py:351
  37.6 2.8 %collective-permute-done.10.refs_1_ = f32[32,1024]{1,0:T(8,128)S(1)} collective-permute-done((f32[32,1024]{1,0:T(8,128)S(1)}, f32[32,1024]{1,0:T(8,128)S(1)}, u32[]{:S(2)}, u32[]{:S(2)}) %collective-permute-start.10) | collective-permute-done | bytes 131104 | tf_op jit(solution)/shard_map/ppermute | solution.py:351
  42.9 1.4 %collective-permute-done.25 = s32[128]{0:T(128)S(1)} collective-permute-done((s32[128]{0:T(128)S(1)}, s32[128]{0:T(128)S(1)}, u32[]{:S(2)}, u32[]{:S(2)}) %collective-permute-start.25) | collective-permute-done | bytes 544 | tf_op jit(solution)/shard_map/ppermute | solution.py:348
  45.0 1.8 %collective-permute-start.17 = (bf16[512,512]{1,0:T(8,128)(2,1)S(1)}, bf16[512,512]{1,0:T(8,128)(2,1)S(1)}, u32[]{:S(2)}, u32[]{:S(2)}) collective-permute-start(bf16[512,512]{1,0:T(8,128)(2,1)S(1)} %get-tuple-element.60), channel_id=1, source_target_pairs={{0,8},{4,12},{8,0},{12,4},{16,24},{20,28},{24,16},{28,20},{1,9},{5... | collective-permute-start | bytes 1572872 | tf_op jit(solution)/shard_map/ppermute | solution.py:351
  46.9 1.6 %collective-permute-start.18 = (bf16[64,256]{1,0:T(8,128)(2,1)S(1)}, bf16[64,256]{1,0:T(8,128)(2,1)S(1)}, u32[]{:S(2)}, u32[]{:S(2)}) collective-permute-start(bf16[64,256]{1,0:T(8,128)(2,1)S(1)} %get-tuple-element.62), channel_id=1, source_target_pairs={{0,1},{1,0},{2,3},{3,2},{4,5},{5,4},{6,7},{7,6},{8,9},{9,8},{10,11... | collective-permute-start | bytes 98312 | tf_op jit(solution)/shard_map/ppermute | solution.py:360
  50.9 2.6 %collective-permute-start.21 = (bf16[64,256]{1,0:T(8,128)(2,1)S(1)}, bf16[64,256]{1,0:T(8,128)(2,1)S(1)}, u32[]{:S(2)}, u32[]{:S(2)}) collective-permute-start(bf16[64,256]{1,0:T(8,128)(2,1)S(1)} %kv_turn.1), channel_id=1, source_target_pairs={{0,2},{1,3},{2,0},{3,1},{4,6},{5,7},{6,4},{7,5},{8,10},{9,11},{10,... | collective-permute-start | bytes 98312 | tf_op jit(solution)/shard_map/ppermute | solution.py:360
  53.7 1.6 %collective-permute-start.20 = (bf16[256,512]{1,0:T(8,128)(2,1)S(1)}, bf16[256,512]{1,0:T(8,128)(2,1)S(1)}, u32[]{:S(2)}, u32[]{:S(2)}) collective-permute-start(bf16[256,512]{1,0:T(8,128)(2,1)S(1)} %q_late.3), channel_id=1, source_target_pairs={{0,16},{4,20},{8,24},{12,28},{16,0},{20,4},{24,8},{28,12},{1,17},{... | collective-permute-start | bytes 786440 | tf_op jit(solution)/shard_map/ppermute | solution.py:351
  56.0 1.8 %collective-permute-start.23 = (bf16[128,256]{1,0:T(8,128)(2,1)S(1)}, bf16[128,256]{1,0:T(8,128)(2,1)S(1)}, u32[]{:S(2)}, u32[]{:S(2)}) collective-permute-start(bf16[128,256]{1,0:T(8,128)(2,1)S(1)} %kv_join.1.refs_0_), channel_id=1, source_target_pairs={{0,16},{4,20},{8,24},{12,28},{16,0},{20,4},{24,8},{28,12},{1,17},{... | collective-permute-start | bytes 196616 | tf_op jit(solution)/shard_map/ppermute | solution.py:351
  57.8 1.4 %collective-permute-start.24 = (bf16[128,256]{1,0:T(8,128)(2,1)S(1)}, bf16[128,256]{1,0:T(8,128)(2,1)S(1)}, u32[]{:S(2)}, u32[]{:S(2)}) collective-permute-start(bf16[128,256]{1,0:T(8,128)(2,1)S(1)} %kv_join.1.refs_0_), channel_id=1, source_target_pairs={{0,24},{4,28},{8,16},{12,20},{16,8},{20,12},{24,0},{28,4},{1,25},{... | collective-permute-start | bytes 196616 | tf_op jit(solution)/shard_map/ppermute | solution.py:351
  61.3 1.6 %collective-permute-start.27 = (bf16[512,512]{1,0:T(8,128)(2,1)S(1)}, bf16[512,512]{1,0:T(8,128)(2,1)S(1)}, u32[]{:S(2)}, u32[]{:S(2)}) collective-permute-start(bf16[512,512]{1,0:T(8,128)(2,1)S(1)} %get-tuple-element.68), channel_id=1, source_target_pairs={{0,8},{4,12},{8,0},{12,4},{16,24},{20,28},{24,16},{28,20},{1,9},{5... | collective-permute-start | bytes 1572872 | tf_op jit(solution)/shard_map/ppermute | solution.py:351
  63.8 2.3 %attend.1.near = bf16[256,512]{1,0:T(8,128)(2,1)S(1)} custom-call(f32[1,128]{1,0:T(1,128)S(1)} %bitcast.14, f32[256,512]{1,0:T(8,128)S(1)} %q_late.2.first, bf16[256,512]{1,0:T(8,128)(2,1)S(1)} %collective-permute-done.20.landed, bf16[128,256]{1,0:T(8,128)(2,1)S(1)} %kv_join.1.refs_0_, bf16[128,256]{1,0:T(8,128)(2,1)S(1)} %collective-permute-done.22.refs_1_, ...), custom_call_target="tpu_custom_call" | custom-call | flops 268435456 | bytes 2097152 | tf_op jit(solution)/shard_map/attend/pallas_call | solution.py:122
  66.1 1.6 %collective-permute-start.28 = (bf16[256,512]{1,0:T(8,128)(2,1)S(1)}, bf16[256,512]{1,0:T(8,128)(2,1)S(1)}, u32[]{:S(2)}, u32[]{:S(2)}) collective-permute-start(bf16[256,512]{1,0:T(8,128)(2,1)S(1)} %attend.1.near), channel_id=1, source_target_pairs={{0,16},{4,20},{8,24},{12,28},{16,0},{20,4},{24,8},{28,12},{1,17},{... | collective-permute-start | bytes 786440 | tf_op jit(solution)/shard_map/ppermute | solution.py:351
  67.7 5.0 %collective-permute-done.28.near = bf16[256,512]{1,0:T(8,128)(2,1)S(1)} collective-permute-done((bf16[256,512]{1,0:T(8,128)(2,1)S(1)}, bf16[256,512]{1,0:T(8,128)(2,1)S(1)}, u32[]{:S(2)}, u32[]{:S(2)}) %collective-permute-start.28) | collective-permute-done | bytes 262176 | tf_op jit(solution)/shard_map/ppermute | solution.py:351
  75.5 1.4 %collective-permute-start.30 = (bf16[128,1024]{1,0:T(8,128)(2,1)S(1)}, bf16[128,1024]{1,0:T(8,128)(2,1)S(1)}, u32[]{:S(2)}, u32[]{:S(2)}) collective-permute-start(bf16[128,1024]{1,0:T(8,128)(2,1)S(1)} %get-tuple-element.70), channel_id=1, source_target_pairs={{0,16},{4,20},{8,24},{12,28},{16,0},{20,4},{24,8},{28,12},{1,17},{... | collective-permute-start | bytes 786440 | tf_op jit(solution)/shard_map/ppermute | solution.py:351
  78.9 5.9 %collective-permute-done.30.landed = bf16[128,1024]{1,0:T(8,128)(2,1)S(1)} collective-permute-done((bf16[128,1024]{1,0:T(8,128)(2,1)S(1)}, bf16[128,1024]{1,0:T(8,128)(2,1)S(1)}, u32[]{:S(2)}, u32[]{:S(2)}) %collective-permute-start.30) | collective-permute-done | bytes 262176 | tf_op jit(solution)/shard_map/ppermute | solution.py:351
  85.4 1.6 %collective-permute-start.31 = (bf16[128,512]{1,0:T(8,128)(2,1)S(1)}, bf16[128,512]{1,0:T(8,128)(2,1)S(1)}, u32[]{:S(2)}, u32[]{:S(2)}) collective-permute-start(bf16[128,512]{1,0:T(8,128)(2,1)S(1)} %get-tuple-element.72), channel_id=1, source_target_pairs={{0,1},{1,0},{2,3},{3,2},{4,5},{5,4},{6,7},{7,6},{8,9},{9,8},{10,11... | collective-permute-start | bytes 393224 | tf_op jit(solution)/shard_map/ppermute | solution.py:360
  87.0 2.6 %collective-permute-start.32 = (bf16[128,512]{1,0:T(8,128)(2,1)S(1)}, bf16[128,512]{1,0:T(8,128)(2,1)S(1)}, u32[]{:S(2)}, u32[]{:S(2)}) collective-permute-start(bf16[128,512]{1,0:T(8,128)(2,1)S(1)} %get-tuple-element.73), channel_id=1, source_target_pairs={{0,2},{1,3},{2,0},{3,1},{4,6},{5,7},{6,4},{7,5},{8,10},{9,11},{10,... | collective-permute-start | bytes 393224 | tf_op jit(solution)/shard_map/ppermute | solution.py:360
  91.9 3.5 %collective-permute-start.37 = (bf16[128,512]{1,0:T(8,128)(2,1)S(1)}, bf16[128,512]{1,0:T(8,128)(2,1)S(1)}, u32[]{:S(2)}, u32[]{:S(2)}) collective-permute-start(bf16[128,512]{1,0:T(8,128)(2,1)S(1)} %get-tuple-element.79), channel_id=1, source_target_pairs={{0,2},{1,3},{2,0},{3,1},{4,6},{5,7},{6,4},{7,5},{8,10},{9,11},{10,... | collective-permute-start | bytes 393224 | tf_op jit(solution)/shard_map/ppermute | solution.py:360
  95.6 4.2 %collective-permute-done.32.refs_2_ = bf16[128,512]{1,0:T(8,128)(2,1)S(1)} collective-permute-done((bf16[128,512]{1,0:T(8,128)(2,1)S(1)}, bf16[128,512]{1,0:T(8,128)(2,1)S(1)}, u32[]{:S(2)}, u32[]{:S(2)}) %collective-permute-start.32) | collective-permute-done | bytes 131104 | tf_op jit(solution)/shard_map/ppermute | solution.py:360
  100.0 9.8 %collective-permute-done.37.refs_2_ = bf16[128,512]{1,0:T(8,128)(2,1)S(1)} collective-permute-done((bf16[128,512]{1,0:T(8,128)(2,1)S(1)}, bf16[128,512]{1,0:T(8,128)(2,1)S(1)}, u32[]{:S(2)}, u32[]{:S(2)}) %collective-permute-start.37) | collective-permute-done | bytes 131104 | tf_op jit(solution)/shard_map/ppermute | solution.py:360
  109.8 1.3 %mix_keep.1 = bf16[128,1024]{1,0:T(8,128)(2,1)} custom-call(s32[3]{0:T(128)S(1)} %pad_add_fusion.1.where, f32[1]{0:T(128)S(6)} %tanh.3.gate, bf16[128,512]{1,0:T(8,128)(2,1)S(1)} %get-tuple-element.44.text, bf16[128,512]{1,0:T(8,128)(2,1)S(1)} %collective-permute-done.34.back, bf16[128,512]{1,0:T(8,128)(2,1)S(1)} %get-tuple-element.77.refs_0_, ...), custom_call_target="tpu_custom_call" | custom-call | flops 1048576 | bytes 1048576 | tf_op jit(solution)/shard_map/mix_keep/pallas_call | solution.py:122
  (93 shorter events, 25.9 us)
Async XLA Ops:
  0.0 21.8 %collective-permute-start.9 = (bf16[512,2048]{1,0:T(8,128)(2,1)}, bf16[512,2048]{1,0:T(8,128)(2,1)S(1)}, u32[]{:S(2)}, u32[]{:S(2)}) collective-permute-start(bf16[512,2048]{1,0:T(8,128)(2,1)} %refs_8_.1), channel_id=1, source_target_pairs={{0,4},{4,0},{8,12},{12,8},{16,20},{20,16},{24,28},{28,24},{1,5},{5... | collective-permute-start | bytes 6291464 | tf_op jit(solution)/shard_map/ppermute | solution.py:348
  0.5 7.0 %collective-permute-start = (bf16[16,4096]{1,0:T(8,128)(2,1)}, bf16[16,4096]{1,0:T(8,128)(2,1)S(1)}, u32[]{:S(2)}, u32[]{:S(2)}) collective-permute-start(bf16[16,4096]{1,0:T(8,128)(2,1)} %bitcast.7), channel_id=1, source_target_pairs={{0,8},{4,12},{8,0},{12,4},{16,24},{20,28},{24,16},{28,20},{1,9},{5... | collective-permute-start | bytes 393224 | tf_op jit(solution)/shard_map/ppermute | solution.py:351
  2.9 8.4 %collective-permute-start.4 = (bf16[16,4096]{1,0:T(8,128)(2,1)}, bf16[16,4096]{1,0:T(8,128)(2,1)S(1)}, u32[]{:S(2)}, u32[]{:S(2)}) collective-permute-start(bf16[16,4096]{1,0:T(8,128)(2,1)} %bitcast.8), channel_id=1, source_target_pairs={{0,24},{4,28},{8,16},{12,20},{16,8},{20,12},{24,0},{28,4},{1,25},{... | collective-permute-start | bytes 393224 | tf_op jit(solution)/shard_map/ppermute | solution.py:351
  11.3 26.3 %collective-permute-start.14 = (bf16[512,1024]{1,0:T(8,128)(2,1)}, bf16[512,1024]{1,0:T(8,128)(2,1)S(1)}, u32[]{:S(2)}, u32[]{:S(2)}) collective-permute-start(bf16[512,1024]{1,0:T(8,128)(2,1)} %q_own.3), channel_id=1, source_target_pairs={{0,8},{4,12},{8,0},{12,4},{16,24},{20,28},{24,16},{28,20},{1,9},{5... | collective-permute-start | bytes 3145736 | tf_op jit(solution)/shard_map/ppermute | solution.py:351
  12.8 5.2 %collective-permute-start.3 = (bf16[16,4096]{1,0:T(8,128)(2,1)}, bf16[16,4096]{1,0:T(8,128)(2,1)S(1)}, u32[]{:S(2)}, u32[]{:S(2)}) collective-permute-start(bf16[16,4096]{1,0:T(8,128)(2,1)} %bitcast.9), channel_id=1, source_target_pairs={{0,16},{4,20},{8,24},{12,28},{16,0},{20,4},{24,8},{28,12},{1,17},{... | collective-permute-start | bytes 393224 | tf_op jit(solution)/shard_map/ppermute | solution.py:351
  18.0 13.7 %collective-permute-start.13 = (bf16[128,2048]{1,0:T(8,128)(2,1)S(1)}, bf16[128,2048]{1,0:T(8,128)(2,1)S(1)}, u32[]{:S(2)}, u32[]{:S(2)}) collective-permute-start(bf16[128,2048]{1,0:T(8,128)(2,1)S(1)} %get-tuple-element.52), channel_id=1, source_target_pairs={{0,16},{4,20},{8,24},{12,28},{16,0},{20,4},{24,8},{28,12},{1,17},{... | collective-permute-start | bytes 1572872 | tf_op jit(solution)/shard_map/ppermute | solution.py:351
  26.2 14.2 %collective-permute-start.10 = (f32[32,1024]{1,0:T(8,128)S(1)}, f32[32,1024]{1,0:T(8,128)S(1)}, u32[]{:S(2)}, u32[]{:S(2)}) collective-permute-start(f32[32,1024]{1,0:T(8,128)S(1)} %get-tuple-element.48), channel_id=1, source_target_pairs={{0,8},{4,12},{8,0},{12,4},{16,24},{20,28},{24,16},{28,20},{1,9},{5... | collective-permute-start | bytes 393224 | tf_op jit(solution)/shard_map/ppermute | solution.py:351
  26.5 13.9 %collective-permute-start.11 = (f32[32,1024]{1,0:T(8,128)S(1)}, f32[32,1024]{1,0:T(8,128)S(1)}, u32[]{:S(2)}, u32[]{:S(2)}) collective-permute-start(f32[32,1024]{1,0:T(8,128)S(1)} %get-tuple-element.49), channel_id=1, source_target_pairs={{0,16},{4,20},{8,24},{12,28},{16,0},{20,4},{24,8},{28,12},{1,17},{... | collective-permute-start | bytes 393224 | tf_op jit(solution)/shard_map/ppermute | solution.py:351
  28.3 13.3 %collective-permute-start.12 = (f32[32,1024]{1,0:T(8,128)S(1)}, f32[32,1024]{1,0:T(8,128)S(1)}, u32[]{:S(2)}, u32[]{:S(2)}) collective-permute-start(f32[32,1024]{1,0:T(8,128)S(1)} %get-tuple-element.50), channel_id=1, source_target_pairs={{0,24},{4,28},{8,16},{12,20},{16,8},{20,12},{24,0},{28,4},{1,25},{... | collective-permute-start | bytes 393224 | tf_op jit(solution)/shard_map/ppermute | solution.py:351
  31.7 15.2 %collective-permute-start.16 = (bf16[512,1024]{1,0:T(8,128)(2,1)S(1)}, bf16[512,1024]{1,0:T(8,128)(2,1)S(1)}, u32[]{:S(2)}, u32[]{:S(2)}) collective-permute-start(bf16[512,1024]{1,0:T(8,128)(2,1)S(1)} %copy-done.1), channel_id=1, source_target_pairs={{0,4},{4,0},{8,12},{12,8},{16,20},{20,16},{24,28},{28,24},{1,5},{5... | collective-permute-start | bytes 3145736 | tf_op jit(solution)/shard_map/ppermute | solution.py:348
  41.6 7.9 %collective-permute-start.15 = (bf16[512,1024]{1,0:T(8,128)(2,1)S(1)}, bf16[512,1024]{1,0:T(8,128)(2,1)S(1)}, u32[]{:S(2)}, u32[]{:S(2)}) collective-permute-start(bf16[512,1024]{1,0:T(8,128)(2,1)S(1)} %collective-permute-done.14.q_side), channel_id=1, source_target_pairs={{0,4},{4,0},{8,12},{12,8},{16,20},{20,16},{24,28},{28,24},{1,5},{5... | collective-permute-start | bytes 3145736 | tf_op jit(solution)/shard_map/ppermute | solution.py:348
  42.3 6.2 %collective-permute-start.19 = (bf16[128,2048]{1,0:T(8,128)(2,1)S(1)}, bf16[128,2048]{1,0:T(8,128)(2,1)S(1)}, u32[]{:S(2)}, u32[]{:S(2)}) collective-permute-start(bf16[128,2048]{1,0:T(8,128)(2,1)S(1)} %collective-permute-done.13.own), channel_id=1, source_target_pairs={{0,4},{4,0},{8,12},{12,8},{16,20},{20,16},{24,28},{28,24},{1,5},{5... | collective-permute-start | bytes 1572872 | tf_op jit(solution)/shard_map/ppermute | solution.py:348
  42.4 15.4 %collective-permute-start.2 = (bf16[128,2048]{1,0:T(8,128)(2,1)S(1)}, bf16[128,2048]{1,0:T(8,128)(2,1)S(1)}, u32[]{:S(2)}, u32[]{:S(2)}) collective-permute-start(bf16[128,2048]{1,0:T(8,128)(2,1)S(1)} %get-tuple-element.46.own), channel_id=1, source_target_pairs={{0,4},{4,0},{8,12},{12,8},{16,20},{20,16},{24,28},{28,24},{1,5},{5... | collective-permute-start | bytes 1572872 | tf_op jit(solution)/shard_map/ppermute | solution.py:348
  45.0 15.3 %collective-permute-start.17 = (bf16[512,512]{1,0:T(8,128)(2,1)S(1)}, bf16[512,512]{1,0:T(8,128)(2,1)S(1)}, u32[]{:S(2)}, u32[]{:S(2)}) collective-permute-start(bf16[512,512]{1,0:T(8,128)(2,1)S(1)} %get-tuple-element.60), channel_id=1, source_target_pairs={{0,8},{4,12},{8,0},{12,4},{16,24},{20,28},{24,16},{28,20},{1,9},{5... | collective-permute-start | bytes 1572872 | tf_op jit(solution)/shard_map/ppermute | solution.py:351
  50.9 4.8 %collective-permute-start.21 = (bf16[64,256]{1,0:T(8,128)(2,1)S(1)}, bf16[64,256]{1,0:T(8,128)(2,1)S(1)}, u32[]{:S(2)}, u32[]{:S(2)}) collective-permute-start(bf16[64,256]{1,0:T(8,128)(2,1)S(1)} %kv_turn.1), channel_id=1, source_target_pairs={{0,2},{1,3},{2,0},{3,1},{4,6},{5,7},{6,4},{7,5},{8,10},{9,11},{10,... | collective-permute-start | bytes 98312 | tf_op jit(solution)/shard_map/ppermute | solution.py:360
  53.7 10.1 %collective-permute-start.20 = (bf16[256,512]{1,0:T(8,128)(2,1)S(1)}, bf16[256,512]{1,0:T(8,128)(2,1)S(1)}, u32[]{:S(2)}, u32[]{:S(2)}) collective-permute-start(bf16[256,512]{1,0:T(8,128)(2,1)S(1)} %q_late.3), channel_id=1, source_target_pairs={{0,16},{4,20},{8,24},{12,28},{16,0},{20,4},{24,8},{28,12},{1,17},{... | collective-permute-start | bytes 786440 | tf_op jit(solution)/shard_map/ppermute | solution.py:351
  55.7 5.6 %collective-permute-start.22 = (bf16[128,256]{1,0:T(8,128)(2,1)S(1)}, bf16[128,256]{1,0:T(8,128)(2,1)S(1)}, u32[]{:S(2)}, u32[]{:S(2)}) collective-permute-start(bf16[128,256]{1,0:T(8,128)(2,1)S(1)} %kv_join.1.refs_0_), channel_id=1, source_target_pairs={{0,8},{4,12},{8,0},{12,4},{16,24},{20,28},{24,16},{28,20},{1,9},{5... | collective-permute-start | bytes 196616 | tf_op jit(solution)/shard_map/ppermute | solution.py:351
  56.0 7.8 %collective-permute-start.23 = (bf16[128,256]{1,0:T(8,128)(2,1)S(1)}, bf16[128,256]{1,0:T(8,128)(2,1)S(1)}, u32[]{:S(2)}, u32[]{:S(2)}) collective-permute-start(bf16[128,256]{1,0:T(8,128)(2,1)S(1)} %kv_join.1.refs_0_), channel_id=1, source_target_pairs={{0,16},{4,20},{8,24},{12,28},{16,0},{20,4},{24,8},{28,12},{1,17},{... | collective-permute-start | bytes 196616 | tf_op jit(solution)/shard_map/ppermute | solution.py:351
  57.8 6.0 %collective-permute-start.24 = (bf16[128,256]{1,0:T(8,128)(2,1)S(1)}, bf16[128,256]{1,0:T(8,128)(2,1)S(1)}, u32[]{:S(2)}, u32[]{:S(2)}) collective-permute-start(bf16[128,256]{1,0:T(8,128)(2,1)S(1)} %kv_join.1.refs_0_), channel_id=1, source_target_pairs={{0,24},{4,28},{8,16},{12,20},{16,8},{20,12},{24,0},{28,4},{1,25},{... | collective-permute-start | bytes 196616 | tf_op jit(solution)/shard_map/ppermute | solution.py:351
  61.3 12.3 %collective-permute-start.27 = (bf16[512,512]{1,0:T(8,128)(2,1)S(1)}, bf16[512,512]{1,0:T(8,128)(2,1)S(1)}, u32[]{:S(2)}, u32[]{:S(2)}) collective-permute-start(bf16[512,512]{1,0:T(8,128)(2,1)S(1)} %get-tuple-element.68), channel_id=1, source_target_pairs={{0,8},{4,12},{8,0},{12,4},{16,24},{20,28},{24,16},{28,20},{1,9},{5... | collective-permute-start | bytes 1572872 | tf_op jit(solution)/shard_map/ppermute | solution.py:351
  66.1 6.6 %collective-permute-start.28 = (bf16[256,512]{1,0:T(8,128)(2,1)S(1)}, bf16[256,512]{1,0:T(8,128)(2,1)S(1)}, u32[]{:S(2)}, u32[]{:S(2)}) collective-permute-start(bf16[256,512]{1,0:T(8,128)(2,1)S(1)} %attend.1.near), channel_id=1, source_target_pairs={{0,16},{4,20},{8,24},{12,28},{16,0},{20,4},{24,8},{28,12},{1,17},{... | collective-permute-start | bytes 786440 | tf_op jit(solution)/shard_map/ppermute | solution.py:351
  72.7 4.9 %collective-permute-start.26 = (bf16[256,512]{1,0:T(8,128)(2,1)S(1)}, bf16[256,512]{1,0:T(8,128)(2,1)S(1)}, u32[]{:S(2)}, u32[]{:S(2)}) collective-permute-start(bf16[256,512]{1,0:T(8,128)(2,1)S(1)} %attend.1.near), channel_id=1, source_target_pairs={{0,4},{4,0},{8,12},{12,8},{16,20},{20,16},{24,28},{28,24},{1,5},{5... | collective-permute-start | bytes 786440 | tf_op jit(solution)/shard_map/ppermute | solution.py:348
  75.5 9.2 %collective-permute-start.30 = (bf16[128,1024]{1,0:T(8,128)(2,1)S(1)}, bf16[128,1024]{1,0:T(8,128)(2,1)S(1)}, u32[]{:S(2)}, u32[]{:S(2)}) collective-permute-start(bf16[128,1024]{1,0:T(8,128)(2,1)S(1)} %get-tuple-element.70), channel_id=1, source_target_pairs={{0,16},{4,20},{8,24},{12,28},{16,0},{20,4},{24,8},{28,12},{1,17},{... | collective-permute-start | bytes 786440 | tf_op jit(solution)/shard_map/ppermute | solution.py:351
  77.0 13.6 %collective-permute-start.35 = (bf16[128,1024]{1,0:T(8,128)(2,1)S(1)}, bf16[128,1024]{1,0:T(8,128)(2,1)S(1)}, u32[]{:S(2)}, u32[]{:S(2)}) collective-permute-start(bf16[128,1024]{1,0:T(8,128)(2,1)S(1)} %get-tuple-element.76), channel_id=1, source_target_pairs={{0,16},{4,20},{8,24},{12,28},{16,0},{20,4},{24,8},{28,12},{1,17},{... | collective-permute-start | bytes 786440 | tf_op jit(solution)/shard_map/ppermute | solution.py:351
  77.6 14.3 %collective-permute-start.1 = (bf16[128,512]{1,0:T(8,128)(2,1)S(1)}, bf16[128,512]{1,0:T(8,128)(2,1)S(1)}, u32[]{:S(2)}, u32[]{:S(2)}) collective-permute-start(bf16[128,512]{1,0:T(8,128)(2,1)S(1)} %get-tuple-element.45), channel_id=1, source_target_pairs={{0,4},{4,0},{8,12},{12,8},{16,20},{20,16},{24,28},{28,24},{1,5},{5... | collective-permute-start | bytes 393224 | tf_op jit(solution)/shard_map/ppermute | solution.py:348
  85.4 10.0 %collective-permute-start.31 = (bf16[128,512]{1,0:T(8,128)(2,1)S(1)}, bf16[128,512]{1,0:T(8,128)(2,1)S(1)}, u32[]{:S(2)}, u32[]{:S(2)}) collective-permute-start(bf16[128,512]{1,0:T(8,128)(2,1)S(1)} %get-tuple-element.72), channel_id=1, source_target_pairs={{0,1},{1,0},{2,3},{3,2},{4,5},{5,4},{6,7},{7,6},{8,9},{9,8},{10,11... | collective-permute-start | bytes 393224 | tf_op jit(solution)/shard_map/ppermute | solution.py:360
  87.0 12.8 %collective-permute-start.32 = (bf16[128,512]{1,0:T(8,128)(2,1)S(1)}, bf16[128,512]{1,0:T(8,128)(2,1)S(1)}, u32[]{:S(2)}, u32[]{:S(2)}) collective-permute-start(bf16[128,512]{1,0:T(8,128)(2,1)S(1)} %get-tuple-element.73), channel_id=1, source_target_pairs={{0,2},{1,3},{2,0},{3,1},{4,6},{5,7},{6,4},{7,5},{8,10},{9,11},{10,... | collective-permute-start | bytes 393224 | tf_op jit(solution)/shard_map/ppermute | solution.py:360
  89.6 10.3 %collective-permute-start.33 = (bf16[128,512]{1,0:T(8,128)(2,1)S(1)}, bf16[128,512]{1,0:T(8,128)(2,1)S(1)}, u32[]{:S(2)}, u32[]{:S(2)}) collective-permute-start(bf16[128,512]{1,0:T(8,128)(2,1)S(1)} %get-tuple-element.74), channel_id=1, source_target_pairs={{0,3},{1,2},{2,1},{3,0},{4,7},{5,6},{6,5},{7,4},{8,11},{9,10},{10,... | collective-permute-start | bytes 393224 | tf_op jit(solution)/shard_map/ppermute | solution.py:360
  91.2 8.9 %collective-permute-start.36 = (bf16[128,512]{1,0:T(8,128)(2,1)S(1)}, bf16[128,512]{1,0:T(8,128)(2,1)S(1)}, u32[]{:S(2)}, u32[]{:S(2)}) collective-permute-start(bf16[128,512]{1,0:T(8,128)(2,1)S(1)} %get-tuple-element.78), channel_id=1, source_target_pairs={{0,1},{1,0},{2,3},{3,2},{4,5},{5,4},{6,7},{7,6},{8,9},{9,8},{10,11... | collective-permute-start | bytes 393224 | tf_op jit(solution)/shard_map/ppermute | solution.py:360
  91.9 17.9 %collective-permute-start.37 = (bf16[128,512]{1,0:T(8,128)(2,1)S(1)}, bf16[128,512]{1,0:T(8,128)(2,1)S(1)}, u32[]{:S(2)}, u32[]{:S(2)}) collective-permute-start(bf16[128,512]{1,0:T(8,128)(2,1)S(1)} %get-tuple-element.79), channel_id=1, source_target_pairs={{0,2},{1,3},{2,0},{3,1},{4,6},{5,7},{6,4},{7,5},{8,10},{9,11},{10,... | collective-permute-start | bytes 393224 | tf_op jit(solution)/shard_map/ppermute | solution.py:360
  95.4 14.4 %collective-permute-start.38 = (bf16[128,512]{1,0:T(8,128)(2,1)S(1)}, bf16[128,512]{1,0:T(8,128)(2,1)S(1)}, u32[]{:S(2)}, u32[]{:S(2)}) collective-permute-start(bf16[128,512]{1,0:T(8,128)(2,1)S(1)} %get-tuple-element.80), channel_id=1, source_target_pairs={{0,3},{1,2},{2,1},{3,0},{4,7},{5,6},{6,5},{7,4},{8,11},{9,10},{10,... | collective-permute-start | bytes 393224 | tf_op jit(solution)/shard_map/ppermute | solution.py:360
  99.9 9.9 %collective-permute-start.34 = (bf16[128,512]{1,0:T(8,128)(2,1)S(1)}, bf16[128,512]{1,0:T(8,128)(2,1)S(1)}, u32[]{:S(2)}, u32[]{:S(2)}) collective-permute-start(bf16[128,512]{1,0:T(8,128)(2,1)S(1)} %mix_give.1), channel_id=1, source_target_pairs={{0,4},{4,0},{8,12},{12,8},{16,20},{20,16},{24,28},{28,24},{1,5},{5... | collective-permute-start | bytes 393224 | tf_op jit(solution)/shard_map/ppermute | solution.py:348
  (18 other events, 153.1 us)
